TPU v7x, 512 devices: a whole 4x4x16 slice. The times are simulated.
512 devices in a mesh: ctx: 32 (over z, core), uly: 16 (over x, y).
Axes of the slice: x: 4, y: 4, z: 16, core: 2. Of those that a mesh axis runs over, the one named last changes fastest.
Arguments:
- queries: bfloat16 [32768, 12288], P(('ctx', 'uly')), may hold values from -8 to 8
- latent: bfloat16 [32768, 576], P(('ctx', 'uly')), may hold values from -8 to 8
- key_up: bfloat16 [512, 8192], P(None, 'uly'), may hold values from -0.25 to 0.25
- value_up: bfloat16 [512, 8192], P(None, 'uly'), may hold values from -0.25 to 0.25
- doc_lengths: int32 [128], replicated, may hold values from 1 to 1024, 32768 in all
Outputs:
- head_out: bfloat16 [32768, 8192], P(('ctx', 'uly'))
Inputs may be any that keep to these rules, and one draw needn't show every extreme that they name: `doc_lengths`: the lengths sum to 32768; the longest document has exactly 1024 tokens.
All inputs are finite; a program needn't handle non-finite values.
Results may differ from a plain program's by a relative error of at most 0.0065.
Values may be sent and summed in bfloat16 or wider, within the bound.
No kernel may reach another device: no remote copies, remote signals or barrier semaphores. Data moves between devices by JAX's collectives and lax.ppermute only.
A program may use at most 64 MiB of HBM per device.

v0:
```python
import math

import jax
import jax.numpy as jnp
from jax import lax
from jax.sharding import PartitionSpec as P

LATENT = 512
ROPE = 64
NOPE = 128
VDIM = 128


def passed_along(block, axis, distance):
    devices = range(lax.axis_size(axis))
    route = [(i - distance, i) for i in devices if i - distance in devices]
    return lax.ppermute(block, axis, route)


def doc_first(doc_lengths, position):
    doc_ends = jnp.cumsum(doc_lengths)
    starts = doc_ends - doc_lengths
    before = starts[None, :] <= position[:, None]
    return jnp.max(jnp.where(before, starts[None, :], 0), axis=1)


def lift_rows(latent_rows, key_up, value_up):
    compact = latent_rows[:, :LATENT]
    key_rows = jnp.dot(compact, key_up, preferred_element_type=jnp.float32).astype(jnp.bfloat16)
    value_rows = jnp.dot(compact, value_up, preferred_element_type=jnp.float32).astype(jnp.bfloat16)
    return (key_rows, value_rows)


def dot_rows(left, right):
    return lax.dot_general(
        left, right, (((1,), (1,)), ((), ())), preferred_element_type=jnp.float32
    )


def per_device(queries, latent, key_up, value_up, doc_lengths):
    uly_count = lax.axis_size("uly")
    block_rows = queries.shape[0] * uly_count
    heads_dev = key_up.shape[1] // NOPE
    score_scale = 1.0 / math.sqrt(NOPE + ROPE)
    local_query = lax.all_to_all(queries, "uly", split_axis=1, concat_axis=0, tiled=True)
    own_latent = lax.all_gather(latent, "uly", axis=0, tiled=True)
    prev_latent = passed_along(own_latent, "ctx", 1)
    both_latent = jnp.concatenate([prev_latent, own_latent], axis=0)
    key_rows, value_rows = lift_rows(both_latent, key_up, value_up)
    rope_rows = both_latent[:, LATENT:]
    block_start = lax.axis_index("ctx") * block_rows
    query_pos = block_start + jnp.arange(block_rows, dtype=jnp.int32)
    key_position = block_start - block_rows + jnp.arange(2 * block_rows, dtype=jnp.int32)
    first_key = doc_first(doc_lengths, query_pos)
    allowed = (key_position[None, :] >= first_key[:, None]) & (
        key_position[None, :] <= query_pos[:, None]
    )

    def softmax_rows(scores):
        scores = jnp.where(allowed, scores, -jnp.inf)
        row_max = jnp.max(scores, axis=1, keepdims=True)
        exp_scores = jnp.exp(scores - row_max)
        return (exp_scores / jnp.sum(exp_scores, axis=1, keepdims=True)).astype(jnp.bfloat16)

    def one_head(head_index):
        query_head = lax.dynamic_slice_in_dim(
            local_query, head_index * (NOPE + ROPE), NOPE + ROPE, 1
        )
        query_nope = query_head[:, :NOPE]
        query_rope = query_head[:, NOPE:]
        key_head = lax.dynamic_slice_in_dim(key_rows, head_index * NOPE, NOPE, 1)
        value_head = lax.dynamic_slice_in_dim(value_rows, head_index * VDIM, VDIM, 1)
        scores = (dot_rows(query_nope, key_head) + dot_rows(query_rope, rope_rows)) * score_scale
        weights = softmax_rows(scores)
        result = jnp.dot(weights, value_head, preferred_element_type=jnp.float32)
        return result.astype(jnp.bfloat16)

    head_outputs = lax.map(one_head, jnp.arange(heads_dev, dtype=jnp.int32))
    merged = jnp.transpose(head_outputs, (1, 0, 2)).reshape(block_rows, heads_dev * VDIM)
    return lax.all_to_all(merged, "uly", split_axis=0, concat_axis=1, tiled=True)


def solution(mesh):
    placed = (P(("ctx", "uly"), None), P(("ctx", "uly"), None), P(None, "uly"), P(None, "uly"), P())
    return jax.shard_map(
        per_device, mesh=mesh, in_specs=placed, out_specs=P(("ctx", "uly"), None), check_vma=False
    )
```

profile of v0, /device:TPU:1, one launch (start us, length us, event | category | flops | bytes accessed | tf_op | source)
XLA Modules:
  0.0 212.3 jit_solution(1808124507691742935)
XLA Ops:
  6.5 0.7 all-gather.2.cloned.1.call-update
  7.3 66.3 %all-gather.2.cloned.1.call-done = bf16[1024,576]{1,0:T(8,128)(2,1)} async-done(((bf16[64,576]{1,0:T(8,128)(2,1)}), bf16[1024,576]{1,0:T(8,128)(2,1)}) %all-gather.2.cloned.1.call-update) | async-done | bytes 1179664 | tf_op jit(solution)/shard_map/all_gather | solution.py:46
  73.6 2.4 %copy.28 = bf16[1024,576]{0,1:T(8,128)(2,1)} copy(bf16[1024,576]{1,0:T(8,128)(2,1)} %all-gather.2.cloned.1.call-done) | data formatting | bytes 2359296 | tf_op jit(solution)/shard_map/all_gather | solution.py:46
  76.0 4.6 %collective-permute-start = (bf16[1024,576]{0,1:T(8,128)(2,1)}, bf16[1024,576]{0,1:T(8,128)(2,1)S(1)}, u32[]{:S(2)}, u32[]{:S(2)}) collective-permute-start(bf16[1024,576]{0,1:T(8,128)(2,1)} %copy.28), channel_id=1, source_target_pairs={{0,16},{16,32},{32,48},{48,64},{64,80},{80,96},{96,112},{112,128},... | collective-permute-start | bytes 3538952 | tf_op jit(solution)/shard_map/ppermute | solution.py:17
  80.6 1.3 copy.36
  81.9 4.8 %all-to-all-start = ((bf16[64,16,768]{2,0,1:T(8,128)(2,1)}), bf16[64,16,768]{2,0,1:T(8,128)(2,1)S(1)}, u32[]{:S(2)}, u32[]{:S(2)}) async-start(bf16[64,16,768]{2,0,1:T(8,128)(2,1)} %bitcast.30), calls=%async_computation | async-start | bytes 3145728 | tf_op jit(solution)/shard_map/all_to_all | solution.py:45
  87.5 6.5 %collective-permute-done = bf16[1024,576]{0,1:T(8,128)(2,1)S(1)} collective-permute-done((bf16[1024,576]{0,1:T(8,128)(2,1)}, bf16[1024,576]{0,1:T(8,128)(2,1)S(1)}, u32[]{:S(2)}, u32[]{:S(2)}) %collective-permute-start) | collective-permute-done | bytes 1179680 | tf_op jit(solution)/shard_map/ppermute | solution.py:17
  94.0 1.4 copy.29
  95.4 1.3 pad_maximum_fusion
  97.3 2.6 %convolution_convert_fusion = bf16[2048,512]{1,0:T(8,128)(2,1)} fusion(bf16[512,512]{1,0:T(8,128)(2,1)S(1)} %copy-done, bf16[1024,576]{1,0:T(8,128)(2,1)S(1)} %copy-done.2, bf16[1024,576]{1,0:T(8,128)(2,1)S(1)} %copy-done.1), kind=kOutput, calls=%fused_computation.17 | convolution fusion | flops 1078984704 | bytes 4980736 | tf_op jit(solution)/shard_map/dot_general | solution.py:30
  99.9 2.7 %convolution_convert_fusion.1 = bf16[2048,512]{1,0:T(8,128)(2,1)} fusion(bf16[512,512]{1,0:T(8,128)(2,1)S(1)} %copy-done.5, bf16[1024,576]{1,0:T(8,128)(2,1)S(1)} %copy-done.2, bf16[1024,576]{1,0:T(8,128)(2,1)S(1)} %copy-done.1), kind=kOutput, calls=%fused_computation.18 | convolution fusion | flops 1078984704 | bytes 4980736 | tf_op jit(solution)/shard_map/dot_general | solution.py:29
  102.6 7.6 %all-to-all-done = bf16[64,16,768]{2,0,1:T(8,128)(2,1)S(1)} async-done(((bf16[64,16,768]{2,0,1:T(8,128)(2,1)}), bf16[64,16,768]{2,0,1:T(8,128)(2,1)S(1)}, u32[]{:S(2)}, u32[]{:S(2)}) %all-to-all-start) | async-done | bytes 1572896 | tf_op jit(solution)/shard_map/all_to_all | solution.py:45
  110.1 71.3 %while.11 = (s32[]{:T(128)}, bf16[4,1024,128]{2,1,0:T(8,128)(2,1)}, s32[4]{0:T(128)S(1)}, bf16[1024,768]{1,0:T(8,128)(2,1)S(1)}, bf16[2048,512]{1,0:T(8,128)(2,1...) while((s32[]{:T(128)}, bf16[4,1024,128]{2,1,0:T(8,128)(2,1)}, ...), condition=%wide.region_5.6_spmd.clone, body=%wide.region_2.5_spmd.clone.sunk | while | flops 1367472128 | bytes 44340000 | solution.py:78
  112.2 5.6 %fusion.34 = f32[1024,2048]{1,0:T(8,128)} fusion(bf16[2048,512]{1,0:T(8,128)(2,1)} %get-tuple-element.208, s32[]{:T(128)S(6)} %select_n.23, bf16[1024,768]{1,0:T(8,128)(2,1)S(1)} %get-tuple-element.207, s32[]{:T(128)S(6)} %select_n.24), kind=kOutput, calls=%fused_computation.10.clone.1 | convolution fusion | flops 536870912 | bytes 9175048 | tf_op jit(solution)/shard_map/while/body/eval_jaxpr/dot_general | solution.py:35
  117.8 5.3 %fusion.35 = (f32[1024]{0:T(1024)S(1)}, f32[1024,2048]{1,0:T(8,128)S(1)}) fusion(f32[1024,2048]{1,0:T(8,128)} %fusion.34, bf16[2048,64]{1,0:T(8,128)(2,1)S(1)} %get-tuple-element.209, bf16[1024,768]{1,0:T(8,128)(2,1)S(1)} %get-tuple-element.207, s32[]{:T(128)S(6)} %add.56, s32[1024]{0:T(1024)S(1)} %get-tuple-element.212, ...), kind=kOutput, calls=%fused_computation.27.clone.1 | convolution fusion | flops 283114496 | bytes 17584132 | tf_op jit(solution)/shard_map/while/body/eval_jaxpr/dot_general | solution.py:35
  123.1 1.3 fusion.36
  124.3 3.6 %fusion.37 = bf16[4,1024,128]{2,1,0:T(8,128)(2,1)} fusion(bf16[4,1024,128]{2,1,0:T(8,128)(2,1)} %get-tuple-element.188, s32[]{:T(128)} %get-tuple-element.187, f32[1024,2048]{1,0:T(8,128)S(1)} %get-tuple-element.168, f32[1024]{0:T(1024)S(1)} %fusion.36, f32[1024]{0:T(1024)S(1)} %get-tuple-element.169, bf16[2048,512]{1,0:T(8,128)(2,1)} %get-tuple-element.210, ...), kind=kOutput, calls=%fused_computation.8.clone.1 | convolution fusion | flops 543293440 | bytes 9183748 | tf_op jit(solution)/shard_map/while/body/eval_jaxpr/dot_general | solution.py:75
  130.0 5.6 %fusion.34 = f32[1024,2048]{1,0:T(8,128)} fusion(bf16[2048,512]{1,0:T(8,128)(2,1)} %get-tuple-element.208, s32[]{:T(128)S(6)} %select_n.23, bf16[1024,768]{1,0:T(8,128)(2,1)S(1)} %get-tuple-element.207, s32[]{:T(128)S(6)} %select_n.24), kind=kOutput, calls=%fused_computation.10.clone.1 | convolution fusion | flops 536870912 | bytes 9175048 | tf_op jit(solution)/shard_map/while/body/eval_jaxpr/dot_general | solution.py:35
  135.6 5.3 %fusion.35 = (f32[1024]{0:T(1024)S(1)}, f32[1024,2048]{1,0:T(8,128)S(1)}) fusion(f32[1024,2048]{1,0:T(8,128)} %fusion.34, bf16[2048,64]{1,0:T(8,128)(2,1)S(1)} %get-tuple-element.209, bf16[1024,768]{1,0:T(8,128)(2,1)S(1)} %get-tuple-element.207, s32[]{:T(128)S(6)} %add.56, s32[1024]{0:T(1024)S(1)} %get-tuple-element.212, ...), kind=kOutput, calls=%fused_computation.27.clone.1 | convolution fusion | flops 283114496 | bytes 17584132 | tf_op jit(solution)/shard_map/while/body/eval_jaxpr/dot_general | solution.py:35
  140.9 1.3 fusion.36
  142.1 3.6 %fusion.37 = bf16[4,1024,128]{2,1,0:T(8,128)(2,1)} fusion(bf16[4,1024,128]{2,1,0:T(8,128)(2,1)} %get-tuple-element.188, s32[]{:T(128)} %get-tuple-element.187, f32[1024,2048]{1,0:T(8,128)S(1)} %get-tuple-element.168, f32[1024]{0:T(1024)S(1)} %fusion.36, f32[1024]{0:T(1024)S(1)} %get-tuple-element.169, bf16[2048,512]{1,0:T(8,128)(2,1)} %get-tuple-element.210, ...), kind=kOutput, calls=%fused_computation.8.clone.1 | convolution fusion | flops 543293440 | bytes 9183748 | tf_op jit(solution)/shard_map/while/body/eval_jaxpr/dot_general | solution.py:75
  147.8 5.6 %fusion.34 = f32[1024,2048]{1,0:T(8,128)} fusion(bf16[2048,512]{1,0:T(8,128)(2,1)} %get-tuple-element.208, s32[]{:T(128)S(6)} %select_n.23, bf16[1024,768]{1,0:T(8,128)(2,1)S(1)} %get-tuple-element.207, s32[]{:T(128)S(6)} %select_n.24), kind=kOutput, calls=%fused_computation.10.clone.1 | convolution fusion | flops 536870912 | bytes 9175048 | tf_op jit(solution)/shard_map/while/body/eval_jaxpr/dot_general | solution.py:35
  153.4 5.3 %fusion.35 = (f32[1024]{0:T(1024)S(1)}, f32[1024,2048]{1,0:T(8,128)S(1)}) fusion(f32[1024,2048]{1,0:T(8,128)} %fusion.34, bf16[2048,64]{1,0:T(8,128)(2,1)S(1)} %get-tuple-element.209, bf16[1024,768]{1,0:T(8,128)(2,1)S(1)} %get-tuple-element.207, s32[]{:T(128)S(6)} %add.56, s32[1024]{0:T(1024)S(1)} %get-tuple-element.212, ...), kind=kOutput, calls=%fused_computation.27.clone.1 | convolution fusion | flops 283114496 | bytes 17584132 | tf_op jit(solution)/shard_map/while/body/eval_jaxpr/dot_general | solution.py:35
  158.7 1.3 fusion.36
  160.0 3.6 %fusion.37 = bf16[4,1024,128]{2,1,0:T(8,128)(2,1)} fusion(bf16[4,1024,128]{2,1,0:T(8,128)(2,1)} %get-tuple-element.188, s32[]{:T(128)} %get-tuple-element.187, f32[1024,2048]{1,0:T(8,128)S(1)} %get-tuple-element.168, f32[1024]{0:T(1024)S(1)} %fusion.36, f32[1024]{0:T(1024)S(1)} %get-tuple-element.169, bf16[2048,512]{1,0:T(8,128)(2,1)} %get-tuple-element.210, ...), kind=kOutput, calls=%fused_computation.8.clone.1 | convolution fusion | flops 543293440 | bytes 9183748 | tf_op jit(solution)/shard_map/while/body/eval_jaxpr/dot_general | solution.py:75
  165.7 5.6 %fusion.34 = f32[1024,2048]{1,0:T(8,128)} fusion(bf16[2048,512]{1,0:T(8,128)(2,1)} %get-tuple-element.208, s32[]{:T(128)S(6)} %select_n.23, bf16[1024,768]{1,0:T(8,128)(2,1)S(1)} %get-tuple-element.207, s32[]{:T(128)S(6)} %select_n.24), kind=kOutput, calls=%fused_computation.10.clone.1 | convolution fusion | flops 536870912 | bytes 9175048 | tf_op jit(solution)/shard_map/while/body/eval_jaxpr/dot_general | solution.py:35
  171.2 5.3 %fusion.35 = (f32[1024]{0:T(1024)S(1)}, f32[1024,2048]{1,0:T(8,128)S(1)}) fusion(f32[1024,2048]{1,0:T(8,128)} %fusion.34, bf16[2048,64]{1,0:T(8,128)(2,1)S(1)} %get-tuple-element.209, bf16[1024,768]{1,0:T(8,128)(2,1)S(1)} %get-tuple-element.207, s32[]{:T(128)S(6)} %add.56, s32[1024]{0:T(1024)S(1)} %get-tuple-element.212, ...), kind=kOutput, calls=%fused_computation.27.clone.1 | convolution fusion | flops 283114496 | bytes 17584132 | tf_op jit(solution)/shard_map/while/body/eval_jaxpr/dot_general | solution.py:35
  176.5 1.3 fusion.36
  177.8 3.6 %fusion.37 = bf16[4,1024,128]{2,1,0:T(8,128)(2,1)} fusion(bf16[4,1024,128]{2,1,0:T(8,128)(2,1)} %get-tuple-element.188, s32[]{:T(128)} %get-tuple-element.187, f32[1024,2048]{1,0:T(8,128)S(1)} %get-tuple-element.168, f32[1024]{0:T(1024)S(1)} %fusion.36, f32[1024]{0:T(1024)S(1)} %get-tuple-element.169, bf16[2048,512]{1,0:T(8,128)(2,1)} %get-tuple-element.210, ...), kind=kOutput, calls=%fused_computation.8.clone.1 | convolution fusion | flops 543293440 | bytes 9183748 | tf_op jit(solution)/shard_map/while/body/eval_jaxpr/dot_general | solution.py:75
  181.4 2.0 copy.31
  183.9 20.5 %all_to_all.38 = bf16[16,64,512]{2,1,0:T(8,128)(2,1)S(1)} all-to-all(bf16[16,64,512]{2,1,0:T(8,128)(2,1)S(1)} %all_to_all.32), channel_id=1, replica_groups=mesh['ctx'=32,'uly'=16] {'uly'}, dimensions={0} | all-to-all | bytes 2097152 | tf_op jit(solution)/shard_map/all_to_all | solution.py:80
  204.4 1.1 copy.34
  (27 shorter events, 4.5 us)
Async XLA Ops:
  6.5 90.2 %copy-start = (bf16[512,512]{1,0:T(8,128)(2,1)S(1)}, bf16[512,512]{1,0:T(8,128)(2,1)}, u32[]{:S(2)}) copy-start(bf16[512,512]{1,0:T(8,128)(2,1)} %param.10) | copy-start | bytes 1572868
  6.5 74.0 %copy-start.3 = (bf16[64,12288]{1,0:T(8,128)(2,1)S(1)}, bf16[64,12288]{1,0:T(8,128)(2,1)}, u32[]{:S(2)}) copy-start(bf16[64,12288]{1,0:T(8,128)(2,1)} %param.7) | copy-start | bytes 4718596
  6.5 67.0 %all-gather.2.cloned.1.call-start = ((), (), s32[]{:S(2)}) async-start(), calls=%async_computation.2 | async-start | bytes 1392640 | tf_op jit(solution)/shard_map/all_gather | solution.py:46
  76.0 18.0 %collective-permute-start = (bf16[1024,576]{0,1:T(8,128)(2,1)}, bf16[1024,576]{0,1:T(8,128)(2,1)S(1)}, u32[]{:S(2)}, u32[]{:S(2)}) collective-permute-start(bf16[1024,576]{0,1:T(8,128)(2,1)} %copy.28), channel_id=1, source_target_pairs={{0,16},{16,32},{32,48},{48,64},{64,80},{80,96},{96,112},{112,128},... | collective-permute-start | bytes 3538952 | tf_op jit(solution)/shard_map/ppermute | solution.py:17
  81.9 4.8 %copy-start.4 = (s32[128]{0:T(128)S(1)}, s32[128]{0:T(128)}, u32[]{:S(2)}) copy-start(s32[128]{0:T(128)} %param.11) | copy-start | bytes 1540
  81.9 28.2 %all-to-all-start = ((bf16[64,16,768]{2,0,1:T(8,128)(2,1)}), bf16[64,16,768]{2,0,1:T(8,128)(2,1)S(1)}, u32[]{:S(2)}, u32[]{:S(2)}) async-start(bf16[64,16,768]{2,0,1:T(8,128)(2,1)} %bitcast.30), calls=%async_computation | async-start | bytes 3145728 | tf_op jit(solution)/shard_map/all_to_all | solution.py:45
  95.4 1.5 copy-start.1
  95.4 1.9 copy-start.2
  97.3 2.6 %copy-start.5 = (bf16[512,512]{1,0:T(8,128)(2,1)S(1)}, bf16[512,512]{1,0:T(8,128)(2,1)}, u32[]{:S(2)}) copy-start(bf16[512,512]{1,0:T(8,128)(2,1)} %param.9) | copy-start | bytes 1572868
Sparse Core Ops, SparseCore 0:
  10.4 63.1 all-gather.1
where the time goes:
time: 214 us; the launch traced here: 212 us
  waiting for transfers between devices  81.1 us (38%)
  matrix products  63.2 us (30%)
  blocking collectives  20.5 us (10%)
  between operations  13.5 us (6%)
  local copies, waits for them, and re-layouts  12 us (6%)
  starting transfers between devices  9.37 us (4%)
  other arithmetic  7 us (3%)
  loops' own time  5.62 us (3%)
    all_gather x1, waiting for transfers between devices, per_device(): own_latent = lax.all_gather(latent, 'uly', axis=0, tiled=True)  66.3 us
    dot_general x8, matrix products, dot_rows(): lax.dot_general(left, right, (((1,), (1,)), ((), ())), preferred_element_...  43.4 us
    all_to_all x1, blocking collectives, per_device(): lax.all_to_all(merged, 'uly', split_axis=0, concat_axis=1, tiled=True)  20.5 us
    dot_general x4, matrix products, one_head(): result = jnp.dot(weights, value_head, preferred_element_type=jnp.float32)  14.6 us
    all_to_all x1, waiting for transfers between devices, per_device(): lax.all_to_all(queries, 'uly', split_axis=1, concat_axis=0, tiled=True)  7.58 us
    ppermute x1, waiting for transfers between devices, passed_along(): return lax.ppermute(block, axis, route)  6.48 us
    another operation x1, loops' own time, per_device(): head_outputs = lax.map(one_head, jnp.arange(heads_dev, dtype=jnp.int32))  5.62 us
    reduce_sum x4, other arithmetic, softmax_rows(): jnp.sum(exp_scores, axis=1, keepdims=True)  5.06 us
  transfers between devices with their start and end apart: 3, of which 3 were waited for; matrix products, arithmetic and copies ran while one was open for 5% of the time, Pallas kernels for 0%

commit v1 on v0

v1 whole, which is shorter than its diff:
```python
import functools
import math

import jax
import jax.numpy as jnp
from jax import lax
from jax.experimental import pallas as pl
from jax.experimental.pallas import tpu as pltpu
from jax.sharding import PartitionSpec as P

LATENT = 512
ROPE = 64
NOPE = 128
VDIM = 128
HEAD = NOPE + ROPE
PAIR = 2 * HEAD
TILE = 256
CODE = 64
FAR = -(2.0**40)
MIB = 1 << 20


def passed_along(block, axis, distance):
    devices = range(lax.axis_size(axis))
    route = [(i - distance, i) for i in devices if i - distance in devices]
    return lax.ppermute(block, axis, route)


def doc_codes(doc_lengths, first, rows):
    position = first + jnp.arange(rows, dtype=jnp.int32)
    ends = jnp.cumsum(doc_lengths)
    doc = jnp.sum((ends[None, :] <= position[:, None]).astype(jnp.int32), axis=1)
    high, low = doc // 8, doc % 8
    lane = jnp.arange(CODE, dtype=jnp.int32)[None, :]
    hot = (lane == high[:, None]) | (lane == 32 + low[:, None])
    used = (lane < 16) | ((lane >= 32) & (lane < 40))
    inside = (position >= 0)[:, None]
    query_code = jnp.where(hot, 1.0, 0.0).astype(jnp.bfloat16)
    key_code = jnp.where(used & ~(hot & inside), FAR, 0.0).astype(jnp.bfloat16)
    return query_code, key_code


def lift_kernel(latent_ref, side_ref, key_up_ref, value_up_ref, *rest):
    key_ref, value_ref = rest[-2:]
    compact = latent_ref[:, :LATENT]
    keys = jnp.dot(compact, key_up_ref[...], preferred_element_type=jnp.float32).astype(jnp.bfloat16)
    values = jnp.dot(compact, value_up_ref[...], preferred_element_type=jnp.float32)
    value_ref[...] = values.astype(jnp.bfloat16)
    rope_code, code_rope = side_ref[:, :128], side_ref[:, 128:]
    left = lax.broadcasted_iota(jnp.int32, rope_code.shape, 1) < CODE
    for head in range(keys.shape[1] // (2 * NOPE)):
        at = head * 2 * NOPE
        first, second = keys[:, at : at + NOPE], keys[:, at + NOPE : at + 2 * NOPE]
        if head % 2 == 0:
            second = rope_code
        else:
            first = jnp.where(left, code_rope, first)
            second = jnp.where(left, second, code_rope)
        key_ref[:, at : at + NOPE] = first
        key_ref[:, at + NOPE : at + 2 * NOPE] = second


def lift(latent_rows, side, key_up, value_up, total_rows, first_row, held=None):
    rows = latent_rows.shape[0]
    key_cols, value_cols = key_up.shape[1], value_up.shape[1]
    first_step = first_row // TILE
    whole = lambda a: pl.BlockSpec(a.shape, lambda i: (0, 0))
    operands = [latent_rows, side, key_up, value_up]
    in_specs = [
        pl.BlockSpec((TILE, latent_rows.shape[1]), lambda i: (i, 0)),
        pl.BlockSpec((TILE, side.shape[1]), lambda i: (i, 0)),
        whole(key_up),
        whole(value_up),
    ]
    aliases = {}
    if held is not None:
        operands += list(held)
        in_specs += [pl.BlockSpec(memory_space=pl.ANY)] * 2
        aliases = {4: 0, 5: 1}
    return pl.pallas_call(
        lift_kernel,
        grid=(rows // TILE,),
        in_specs=in_specs,
        out_specs=[
            pl.BlockSpec((TILE, key_cols), lambda i: (first_step + i, 0)),
            pl.BlockSpec((TILE, value_cols), lambda i: (first_step + i, 0)),
        ],
        out_shape=[
            jax.ShapeDtypeStruct((total_rows, key_cols), jnp.bfloat16),
            jax.ShapeDtypeStruct((total_rows, value_cols), jnp.bfloat16),
        ],
        input_output_aliases=aliases,
        compiler_params=pltpu.CompilerParams(vmem_limit_bytes=16 * MIB),
        cost_estimate=pl.CostEstimate(
            flops=2 * rows * LATENT * (key_cols + value_cols),
            bytes_accessed=2 * rows * (key_cols + value_cols + 768),
            transcendentals=0,
        ),
        name="lift",
    )(*operands)


def attend_kernel(window, query_ref, code_ref, key_ref, value_ref, out_ref):
    to_log2 = math.log2(math.e) / math.sqrt(HEAD)
    left = lax.broadcasted_iota(jnp.int32, (TILE, 128), 1) < CODE
    causal = lax.broadcasted_iota(jnp.int32, (TILE, TILE), 1) <= lax.broadcasted_iota(
        jnp.int32, (TILE, TILE), 0
    )
    ones = jnp.ones((window, 128), jnp.bfloat16)

    @pl.loop(0, query_ref.shape[0] // TILE)
    def _(step):
        begin = pl.multiple_of(step * TILE, TILE)
        rows = pl.ds(begin, TILE)
        span = pl.ds(begin, window)
        code = code_ref[rows, :]
        for head in range(2):
            if head == 0:
                query = jnp.concatenate(
                    [query_ref[rows, :128], jnp.where(left, query_ref[rows, 128:256], code)], axis=1
                )
            else:
                query = jnp.concatenate(
                    [jnp.where(left, code, query_ref[rows, 128:256]), query_ref[rows, 256:384]], axis=1
                )
            keys = key_ref[span, head * 256 : (head + 1) * 256]
            scores = lax.dot_general(
                query, keys, (((1,), (1,)), ((), ())), preferred_element_type=jnp.float32
            )
            own = jnp.where(causal, scores[:, window - TILE :], FAR)
            scores = jnp.concatenate([scores[:, : window - TILE], own], axis=1)
            top = jnp.max(scores, axis=1, keepdims=True) * to_log2
            weights = jnp.exp2(scores * to_log2 - top).astype(jnp.bfloat16)
            values = jnp.concatenate(
                [value_ref[span, head * VDIM : (head + 1) * VDIM], ones], axis=1
            )
            total = jnp.dot(weights, values, preferred_element_type=jnp.float32)
            result = total[:, :VDIM] / total[:, VDIM:]
            out_ref[rows, head * VDIM : (head + 1) * VDIM] = result.astype(jnp.bfloat16)


def attend(query, code, keys, values):
    rows, total = query.shape[0], keys.shape[0]
    pairs = query.shape[1] // PAIR
    window = total - rows + TILE
    return pl.pallas_call(
        functools.partial(attend_kernel, window),
        grid=(pairs,),
        in_specs=[
            pl.BlockSpec((rows, PAIR), lambda i: (0, i)),
            pl.BlockSpec(code.shape, lambda i: (0, 0)),
            pl.BlockSpec((total, 4 * NOPE), lambda i: (0, i)),
            pl.BlockSpec((total, 2 * VDIM), lambda i: (0, i)),
        ],
        out_specs=pl.BlockSpec((rows, 2 * VDIM), lambda i: (0, i)),
        out_shape=jax.ShapeDtypeStruct((rows, pairs * 2 * VDIM), jnp.bfloat16),
        compiler_params=pltpu.CompilerParams(vmem_limit_bytes=40 * MIB),
        cost_estimate=pl.CostEstimate(
            flops=4 * rows * window * pairs * 512,
            bytes_accessed=2 * (total * pairs * 768 + rows * pairs * 640),
            transcendentals=2 * pairs * rows * window,
        ),
        name="attend",
    )(query, code, keys, values)


def per_device(queries, latent, key_up, value_up, doc_lengths):
    uly_count = lax.axis_size("uly")
    own_rows = queries.shape[0]
    block_rows = own_rows * uly_count
    heads_dev = key_up.shape[1] // NOPE
    block_start = lax.axis_index("ctx") * block_rows
    pads = [(0, NOPE) if head % 2 == 0 else (CODE, ROPE) for head in range(heads_dev)]
    wide_up = jnp.concatenate(
        [jnp.pad(key_up[:, h * NOPE : (h + 1) * NOPE], ((0, 0), pads[h])) for h in range(heads_dev)],
        axis=1,
    )
    query_code, key_code = doc_codes(doc_lengths, block_start - block_rows, 2 * block_rows)
    query_code = query_code[block_rows:]
    both_codes = jnp.concatenate([query_code, query_code], axis=1)

    copies = jnp.broadcast_to(latent[None], (uly_count,) + latent.shape)
    own = lax.all_to_all(copies, "uly", split_axis=0, concat_axis=0)
    own = own.reshape(block_rows, latent.shape[1])
    previous = passed_along(own, "ctx", 1)
    local_query = lax.all_to_all(queries, "uly", split_axis=1, concat_axis=0, tiled=True)

    def side_of(rows, code):
        rope = rows[:, LATENT:]
        return jnp.concatenate([rope, code, code, rope], axis=1)

    held = lift(own, side_of(own, key_code[block_rows:]), wide_up, value_up, 2 * block_rows, block_rows)
    keys, values = lift(
        previous, side_of(previous, key_code[:block_rows]), wide_up, value_up, 2 * block_rows, 0, held
    )
    result = attend(local_query, both_codes, keys, values)
    result = result.reshape(uly_count, own_rows, heads_dev * VDIM)
    result = lax.all_to_all(result, "uly", split_axis=0, concat_axis=0)
    return jnp.transpose(result, (1, 0, 2)).reshape(own_rows, uly_count * heads_dev * VDIM)


def solution(mesh):
    placed = (P(("ctx", "uly"), None), P(("ctx", "uly"), None), P(None, "uly"), P(None, "uly"), P())
    return jax.shard_map(
        per_device, mesh=mesh, in_specs=placed, out_specs=P(("ctx", "uly"), None), check_vma=False
    )
```

time: 214 us -> 108 us (0.50)
  the two profiles are of different devices: /device:TPU:1 before, /device:TPU:96 now
where the time goes in v1:
time: 108 us
  blocking collectives  24.9 us (23%)
  local copies, waits for them, and re-layouts  23.6 us (22%)
  waiting for transfers between devices  22.2 us (21%)
  Pallas kernels  17.2 us (16%)
  starting transfers between devices  13.4 us (12%)
  other arithmetic  6.04 us (6%)
    all_to_all x1, blocking collectives, per_device(): result = lax.all_to_all(result, 'uly', split_axis=0, concat_axis=0)  24.9 us
    all_to_all x1, waiting for transfers between devices, per_device(): own = lax.all_to_all(copies, 'uly', split_axis=0, concat_axis=0)  16.1 us
    unnamed x28, local copies, waits for them, and re-layouts  14.2 us
    pallas_call x1, Pallas kernels, attend(): pl.pallas_call(functools.partial(attend_kernel, window), grid=(pairs,), i...  12.5 us
    all_to_all x1, starting transfers between devices, per_device(): own = lax.all_to_all(copies, 'uly', split_axis=0, concat_axis=0)  7.03 us
    ppermute x1, waiting for transfers between devices, passed_along(): return lax.ppermute(block, axis, route)  6.15 us
    pallas_call x2, Pallas kernels, lift(): pl.pallas_call(lift_kernel, grid=(rows // TILE,), in_specs=in_specs, out_...  4.69 us
    all_to_all x1, starting transfers between devices, per_device(): lax.all_to_all(queries, 'uly', split_axis=1, concat_axis=0, tiled=True)  4.41 us
  transfers between devices with their start and end apart: 3, of which 2 were waited for; matrix products, arithmetic and copies ran while one was open for 11% of the time, Pallas kernels for 4%

profile of v1, /device:TPU:96, one launch (start us, length us, event | category | flops | bytes accessed | tf_op | source)
XLA Modules:
  0.0 107.6 jit_solution(11858318825015609725)
XLA Ops:
  0.0 2.2 %broadcast_in_dim.26 = bf16[16,64,576]{2,1,0:T(8,128)(2,1)} broadcast(bf16[64,576]{1,0:T(8,128)(2,1)} %param.6), dimensions={1,2} | broadcast | bytes 1253376 | tf_op jit(solution)/shard_map/broadcast_in_dim | solution.py:182
  2.2 7.0 %all-to-all-start.1 = ((bf16[16,64,576]{2,1,0:T(8,128)(2,1)}), bf16[16,64,576]{2,1,0:T(8,128)(2,1)S(1)}, u32[]{:S(2)}, u32[]{:S(2)}) async-start(bf16[16,64,576]{2,1,0:T(8,128)(2,1)} %broadcast_in_dim.26), calls=%async_computation.1 | async-start | bytes 2621440 | tf_op jit(solution)/shard_map/all_to_all | solution.py:183
  9.4 0.2 reduce-window.8
  9.7 0.6 convert_reduce_fusion
  10.4 1.2 %fusion.8 = pred[2048,64]{1,0:T(8,128)(4,1)S(1)} fusion(s32[2048]{0:T(1024)S(1)} %get-tuple-element.19, s32[2048]{0:T(1024)S(1)} %get-tuple-element.18), kind=kLoop, calls=%fused_computation.18 | loop fusion | flops 393216 | bytes 147456 | tf_op jit(solution)/shard_map/or | solution.py:35
  11.6 1.3 %copy.29 = bf16[8,16,8,768]{3,2,0,1:T(8,128)(2,1)} copy(bf16[8,16,8,768]{3,2,1,0:T(8,128)(2,1)S(1)} %bitcast.18) | data formatting | bytes 3145728 | tf_op jit(solution)/shard_map/all_to_all | solution.py:186
  13.0 0.1 pad_maximum_fusion.2.code_ref
  13.2 0.8 fusion.13
  14.0 16.1 %all-to-all-done.1 = bf16[16,64,576]{2,1,0:T(8,128)(2,1)S(1)} async-done(((bf16[16,64,576]{2,1,0:T(8,128)(2,1)}), bf16[16,64,576]{2,1,0:T(8,128)(2,1)S(1)}, u32[]{:S(2)}, u32[]{:S(2)}) %all-to-all-start.1) | async-done | bytes 1179680 | tf_op jit(solution)/shard_map/all_to_all | solution.py:183
  30.1 4.4 %all-to-all-start = ((bf16[64,16,768]{2,0,1:T(8,128)(2,1)}), bf16[64,16,768]{2,0,1:T(8,128)(2,1)}, u32[]{:S(2)}, u32[]{:S(2)}) async-start(bf16[64,16,768]{2,0,1:T(8,128)(2,1)} %bitcast.12), calls=%async_computation | async-start | bytes 3145728 | tf_op jit(solution)/shard_map/all_to_all | solution.py:186
  34.5 1.5 %copy.22 = bf16[1024,576]{0,1:T(8,128)(2,1)} copy(bf16[1024,576]{1,0:T(8,128)(2,1)S(1)} %bitcast.13) | data formatting | bytes 2359296 | tf_op jit(solution)/shard_map/reshape | solution.py:184
  36.0 1.9 %collective-permute-start = (bf16[1024,576]{0,1:T(8,128)(2,1)}, bf16[1024,576]{0,1:T(8,128)(2,1)}, u32[]{:S(2)}, u32[]{:S(2)}) collective-permute-start(bf16[1024,576]{0,1:T(8,128)(2,1)} %copy.22), channel_id=1, source_target_pairs={{0,16},{16,32},{32,48},{48,64},{64,80},{80,96},{96,112},{112,128},... | collective-permute-start | bytes 3538952 | tf_op jit(solution)/shard_map/ppermute | solution.py:26
  37.9 1.7 %select_convert_fusion = bf16[2048,64]{1,0:T(8,128)(2,1)S(1)} fusion(pred[2048]{0:T(1024)(128)(4,1)S(1)} %broadcast_compare_fusion, pred[64]{0:T(512)(128)(4,1)S(1)} %and_or_fusion, s32[2048]{0:T(1024)S(1)} %get-tuple-element.19, s32[2048]{0:T(1024)S(1)} %get-tuple-element.18), kind=kLoop, calls=%fused_computation.14 | loop fusion | flops 1048576 | bytes 280640 | tf_op jit(solution)/shard_map/convert_element_type | solution.py:39
  39.6 0.7 fusion.12
  40.4 1.2 %fusion.6.key_up_ref = bf16[512,1024]{1,0:T(8,128)(2,1)S(1)} fusion(bf16[512,128]{1,0:T(8,128)(2,1)} %get-tuple-element.16, bf16[512,128]{1,0:T(8,128)(2,1)} %get-tuple-element.17, bf16[512,128]{1,0:T(8,128)(2,1)S(1)} %get-tuple-element.15, bf16[512,256]{1,0:T(8,128)(2,1)S(1)} %slice_select_fusion), kind=kLoop, calls=%fused_computation.12 | loop fusion | flops 9437184 | bytes 1703936 | tf_op jit(solution)/shard_map/concatenate | solution.py:174
  41.6 0.4 pad_maximum_fusion.1.side_ref
  42.0 2.4 %lift.2 = (bf16[2048,1024]{1,0:T(8,128)(2,1)S(1)}, bf16[2048,512]{1,0:T(8,128)(2,1)S(1)}) custom-call(bf16[1024,576]{1,0:T(8,128)(2,1)S(1)} %bitcast.15, bf16[1024,256]{1,0:T(8,128)(2,1)S(1)} %pad_maximum_fusion.1.side_ref, bf16[512,1024]{1,0:T(8,128)(2,1)S(1)} %fusion.6.key_up_ref, bf16[512,512]{1,0:T(8,128)(2,1)S(1)} %copy-done.8), custom_call_target="tpu_custom_call" | custom-call | flops 1610612736 | bytes 4718592 | tf_op jit(solution)/shard_map/lift/pallas_call | solution.py:80
  44.3 1.9 %copy-done = bf16[2048,1024]{1,0:T(8,128)(2,1)} copy-done((bf16[2048,1024]{1,0:T(8,128)(2,1)}, bf16[2048,1024]{1,0:T(8,128)(2,1)S(1)}, u32[]{:S(2)}) %copy-start) | copy-done | bytes 4194328
  46.3 1.3 %copy-done.4 = bf16[2048,512]{1,0:T(8,128)(2,1)} copy-done((bf16[2048,512]{1,0:T(8,128)(2,1)}, bf16[2048,512]{1,0:T(8,128)(2,1)S(1)}, u32[]{:S(2)}) %copy-start.4) | copy-done | bytes 2097176
  47.6 6.2 %collective-permute-done = bf16[1024,576]{0,1:T(8,128)(2,1)} collective-permute-done((bf16[1024,576]{0,1:T(8,128)(2,1)}, bf16[1024,576]{0,1:T(8,128)(2,1)}, u32[]{:S(2)}, u32[]{:S(2)}) %collective-permute-start) | collective-permute-done | bytes 1179680 | tf_op jit(solution)/shard_map/ppermute | solution.py:26
  53.8 1.7 %copy.24.latent_ref = bf16[1024,576]{1,0:T(8,128)(2,1)S(1)} copy(bf16[1024,576]{0,1:T(8,128)(2,1)} %collective-permute-done) | data formatting | bytes 2359296 | tf_op jit(solution)/shard_map/ppermute | solution.py:26
  55.5 0.4 pad_maximum_fusion.side_ref
  55.9 2.2 %copy-done.1 = bf16[2048,1024]{1,0:T(8,128)(2,1)S(1)} copy-done((bf16[2048,1024]{1,0:T(8,128)(2,1)S(1)}, bf16[2048,1024]{1,0:T(8,128)(2,1)}, u32[]{:S(2)}) %copy-start.1) | copy-done | bytes 4194328
  58.1 1.6 %copy-done.5 = bf16[2048,512]{1,0:T(8,128)(2,1)S(1)} copy-done((bf16[2048,512]{1,0:T(8,128)(2,1)S(1)}, bf16[2048,512]{1,0:T(8,128)(2,1)}, u32[]{:S(2)}) %copy-start.5) | copy-done | bytes 2097176
  59.6 2.3 %lift.3 = (bf16[2048,1024]{1,0:T(8,128)(2,1)S(1)}, bf16[2048,512]{1,0:T(8,128)(2,1)S(1)}) custom-call(bf16[1024,576]{1,0:T(8,128)(2,1)S(1)} %copy.24.latent_ref, bf16[1024,256]{1,0:T(8,128)(2,1)S(1)} %pad_maximum_fusion.side_ref, bf16[512,1024]{1,0:T(8,128)(2,1)S(1)} %fusion.6.key_up_ref, ...), custom_call_target="tpu_custom_call", output_to_operand_aliasing={{0}: (4, {}), {1}: (5, {})} | custom-call | flops 1610612736 | bytes 4718592 | tf_op jit(solution)/shard_map/lift/pallas_call | solution.py:80
  62.0 1.9 %copy-done.2 = bf16[2048,1024]{1,0:T(8,128)(2,1)} copy-done((bf16[2048,1024]{1,0:T(8,128)(2,1)}, bf16[2048,1024]{1,0:T(8,128)(2,1)S(1)}, u32[]{:S(2)}) %copy-start.2) | copy-done | bytes 4194328
  63.9 1.3 %copy-done.6 = bf16[2048,512]{1,0:T(8,128)(2,1)} copy-done((bf16[2048,512]{1,0:T(8,128)(2,1)}, bf16[2048,512]{1,0:T(8,128)(2,1)S(1)}, u32[]{:S(2)}) %copy-start.6) | copy-done | bytes 2097176
  65.3 2.2 %copy-done.3 = bf16[2048,1024]{1,0:T(8,128)(2,1)S(1)} copy-done((bf16[2048,1024]{1,0:T(8,128)(2,1)S(1)}, bf16[2048,1024]{1,0:T(8,128)(2,1)}, u32[]{:S(2)}) %copy-start.3) | copy-done | bytes 4194328
  67.5 1.6 %copy-done.7 = bf16[2048,512]{1,0:T(8,128)(2,1)S(1)} copy-done((bf16[2048,512]{1,0:T(8,128)(2,1)S(1)}, bf16[2048,512]{1,0:T(8,128)(2,1)}, u32[]{:S(2)}) %copy-start.7) | copy-done | bytes 2097176
  69.1 12.5 %attend.1 = bf16[1024,512]{1,0:T(8,128)(2,1)S(1)} custom-call(bf16[1024,768]{1,0:T(8,128)(2,1)} %bitcast.1.query_ref, bf16[1024,128]{1,0:T(8,128)(2,1)S(1)} %pad_maximum_fusion.2.code_ref, bf16[2048,1024]{1,0:T(8,128)(2,1)S(1)} %copy-done.3, bf16[2048,512]{1,0:T(8,128)(2,1)S(1)} %copy-done.7), custom_call_target="tpu_custom_call" | custom-call | flops 5368709120 | bytes 8912896 | tf_op jit(solution)/shard_map/attend/pallas_call | solution.py:146
  81.6 24.9 %all_to_all.29 = bf16[16,64,512]{2,1,0:T(8,128)(2,1)S(1)} all-to-all(bf16[16,64,512]{2,1,0:T(8,128)(2,1)S(1)} %bitcast.16), channel_id=1, replica_groups=mesh['ctx'=32,'uly'=16] {'uly'}, dimensions={0} | all-to-all | bytes 2097152 | tf_op jit(solution)/shard_map/all_to_all | solution.py:198
  106.5 1.1 copy.27
  (31 shorter events, 0.4 us)
Async XLA Ops:
  0.0 9.3 %copy-start.12 = (s32[128]{0:T(128)S(1)}, s32[128]{0:T(128)}, u32[]{:S(2)}) copy-start(s32[128]{0:T(128)} %param.9) | copy-start | bytes 1540
  0.0 11.6 %copy-start.9 = (bf16[64,12288]{1,0:T(8,128)(2,1)S(1)}, bf16[64,12288]{1,0:T(8,128)(2,1)}, u32[]{:S(2)}) copy-start(bf16[64,12288]{1,0:T(8,128)(2,1)} %param.5) | copy-start | bytes 4718596
  2.2 27.8 %all-to-all-start.1 = ((bf16[16,64,576]{2,1,0:T(8,128)(2,1)}), bf16[16,64,576]{2,1,0:T(8,128)(2,1)S(1)}, u32[]{:S(2)}, u32[]{:S(2)}) async-start(bf16[16,64,576]{2,1,0:T(8,128)(2,1)} %broadcast_in_dim.26), calls=%async_computation.1 | async-start | bytes 2621440 | tf_op jit(solution)/shard_map/all_to_all | solution.py:183
  11.6 1.6 %copy-start.11 = (bf16[512,512]{1,0:T(8,128)(2,1)S(1)}, bf16[512,512]{1,0:T(8,128)(2,1)}, u32[]{:S(2)}) copy-start(bf16[512,512]{1,0:T(8,128)(2,1)} %param.7) | copy-start | bytes 1572868
  11.6 2.4 %copy-start.13 = (pred[256]{0:T(512)(128)(4,1)S(1)}, pred[256]{0:T(512)(128)(4,1)}, u32[]{:S(2)}) copy-start(pred[256]{0:T(512)(128)(4,1)} %constant.58.clone.1) | copy-start | bytes 772
  30.1 35.2 %all-to-all-start = ((bf16[64,16,768]{2,0,1:T(8,128)(2,1)}), bf16[64,16,768]{2,0,1:T(8,128)(2,1)}, u32[]{:S(2)}, u32[]{:S(2)}) async-start(bf16[64,16,768]{2,0,1:T(8,128)(2,1)} %bitcast.12), calls=%async_computation | async-start | bytes 3145728 | tf_op jit(solution)/shard_map/all_to_all | solution.py:186
  36.0 17.8 %collective-permute-start = (bf16[1024,576]{0,1:T(8,128)(2,1)}, bf16[1024,576]{0,1:T(8,128)(2,1)}, u32[]{:S(2)}, u32[]{:S(2)}) collective-permute-start(bf16[1024,576]{0,1:T(8,128)(2,1)} %copy.22), channel_id=1, source_target_pairs={{0,16},{16,32},{32,48},{48,64},{64,80},{80,96},{96,112},{112,128},... | collective-permute-start | bytes 3538952 | tf_op jit(solution)/shard_map/ppermute | solution.py:26
  39.6 2.4 %copy-start.8 = (bf16[512,512]{1,0:T(8,128)(2,1)S(1)}, bf16[512,512]{1,0:T(8,128)(2,1)}, u32[]{:S(2)}) copy-start(bf16[512,512]{1,0:T(8,128)(2,1)} %value_up_ref.3) | copy-start | bytes 1572868
  44.3 2.0 %copy-start = (bf16[2048,1024]{1,0:T(8,128)(2,1)}, bf16[2048,1024]{1,0:T(8,128)(2,1)S(1)}, u32[]{:S(2)}) copy-start(bf16[2048,1024]{1,0:T(8,128)(2,1)S(1)} %get-tuple-element.9.rest_0_) | copy-start | bytes 12582916
  46.3 1.3 %copy-start.4 = (bf16[2048,512]{1,0:T(8,128)(2,1)}, bf16[2048,512]{1,0:T(8,128)(2,1)S(1)}, u32[]{:S(2)}) copy-start(bf16[2048,512]{1,0:T(8,128)(2,1)S(1)} %get-tuple-element.10.rest_1_) | copy-start | bytes 6291460
  47.6 7.9 %copy-start.10 = (bf16[1024,64]{1,0:T(8,128)(2,1)S(1)}, bf16[1024,64]{1,0:T(8,128)(2,1)}, u32[]{:S(2)}) copy-start(bf16[1024,64]{1,0:T(8,128)(2,1)} %get-tuple-element.14) | copy-start | bytes 393220
  55.9 2.2 %copy-start.1 = (bf16[2048,1024]{1,0:T(8,128)(2,1)S(1)}, bf16[2048,1024]{1,0:T(8,128)(2,1)}, u32[]{:S(2)}) copy-start(bf16[2048,1024]{1,0:T(8,128)(2,1)} %copy-done) | copy-start | bytes 12582916
  58.1 1.6 %copy-start.5 = (bf16[2048,512]{1,0:T(8,128)(2,1)S(1)}, bf16[2048,512]{1,0:T(8,128)(2,1)}, u32[]{:S(2)}) copy-start(bf16[2048,512]{1,0:T(8,128)(2,1)} %copy-done.4) | copy-start | bytes 6291460
  62.0 2.0 %copy-start.2 = (bf16[2048,1024]{1,0:T(8,128)(2,1)}, bf16[2048,1024]{1,0:T(8,128)(2,1)S(1)}, u32[]{:S(2)}) copy-start(bf16[2048,1024]{1,0:T(8,128)(2,1)S(1)} %get-tuple-element.11.key_ref) | copy-start | bytes 12582916
  63.9 1.3 %copy-start.6 = (bf16[2048,512]{1,0:T(8,128)(2,1)}, bf16[2048,512]{1,0:T(8,128)(2,1)S(1)}, u32[]{:S(2)}) copy-start(bf16[2048,512]{1,0:T(8,128)(2,1)S(1)} %get-tuple-element.12.value_ref) | copy-start | bytes 6291460
  65.3 2.2 %copy-start.3 = (bf16[2048,1024]{1,0:T(8,128)(2,1)S(1)}, bf16[2048,1024]{1,0:T(8,128)(2,1)}, u32[]{:S(2)}) copy-start(bf16[2048,1024]{1,0:T(8,128)(2,1)} %copy-done.2) | copy-start | bytes 12582916
  67.5 1.6 %copy-start.7 = (bf16[2048,512]{1,0:T(8,128)(2,1)S(1)}, bf16[2048,512]{1,0:T(8,128)(2,1)}, u32[]{:S(2)}) copy-start(bf16[2048,512]{1,0:T(8,128)(2,1)} %copy-done.6) | copy-start | bytes 6291460

commit v2 on v1

v2 whole, which is shorter than its diff:
```python
import functools
import math

import jax
import jax.numpy as jnp
from jax import lax
from jax.experimental import pallas as pl
from jax.experimental.pallas import tpu as pltpu
from jax.sharding import PartitionSpec as P

LATENT = 512
ROPE = 64
NOPE = 128
VDIM = 128
HEAD = NOPE + ROPE
PAIR = 2 * HEAD
WIDE = LATENT + 2 * ROPE
TILE = 256
CODE = 64
FAR = -(2.0**40)
MIB = 1 << 20


def passed_along(block, axis, distance):
    devices = range(lax.axis_size(axis))
    route = [(i - distance, i) for i in devices if i - distance in devices]
    return lax.ppermute(block, axis, route)


def doc_codes(doc_lengths, first, rows):
    position = first + jnp.arange(rows, dtype=jnp.int32)
    ends = jnp.cumsum(doc_lengths)
    doc = jnp.sum((ends[None, :] <= position[:, None]).astype(jnp.int32), axis=1)
    high, low = doc // 8, doc % 8
    lane = (jnp.arange(2 * CODE, dtype=jnp.int32) % CODE)[None, :]
    hot = (lane == high[:, None]) | (lane == 32 + low[:, None])
    used = (lane < 16) | ((lane >= 32) & (lane < 40))
    inside = (position >= 0)[:, None]
    query_code = jnp.where(hot, 1.0, 0.0).astype(jnp.bfloat16)
    key_code = jnp.where(used & ~(hot & inside), FAR, 0.0).astype(jnp.bfloat16)
    return query_code, key_code


def first_tiles(doc_lengths, block_start, block_rows):
    starts = jnp.cumsum(doc_lengths) - doc_lengths
    position = block_start + TILE * jnp.arange(block_rows // TILE, dtype=jnp.int32)
    before = starts[None, :] <= position[:, None]
    first_key = jnp.max(jnp.where(before, starts[None, :], 0), axis=1)
    return (first_key - (block_start - block_rows)) // TILE


def spread_kernel(latent_ref, copies_ref, wide, sems):
    wide[:, :LATENT] = latent_ref[:, :LATENT]
    rope = latent_ref[:, LATENT:]
    wide[:, LATENT:] = jnp.concatenate([rope, rope], axis=1)
    copies = [
        pltpu.make_async_copy(wide, copies_ref.at[i], sems.at[i]) for i in range(copies_ref.shape[0])
    ]
    for copy in copies:
        copy.start()
    for copy in copies:
        copy.wait()


def spread(latent, count):
    rows = latent.shape[0]
    return pl.pallas_call(
        spread_kernel,
        in_specs=[pl.BlockSpec(memory_space=pltpu.VMEM)],
        out_specs=pl.BlockSpec(memory_space=pl.ANY),
        out_shape=jax.ShapeDtypeStruct((count, rows, WIDE), latent.dtype),
        scratch_shapes=[pltpu.VMEM((rows, WIDE), latent.dtype), pltpu.SemaphoreType.DMA((count,))],
        compiler_params=pltpu.CompilerParams(vmem_limit_bytes=60 * MIB),
        name="spread",
    )(latent)


def lift_kernel(latent_ref, code_ref, key_up_ref, value_up_ref, key_ref, value_ref):
    compact = latent_ref[:, :LATENT]
    keys = jnp.dot(compact, key_up_ref[...], preferred_element_type=jnp.float32).astype(jnp.bfloat16)
    values = jnp.dot(compact, value_up_ref[...], preferred_element_type=jnp.float32)
    value_ref[...] = values.astype(jnp.bfloat16)
    rope, code = latent_ref[:, LATENT:], code_ref[...]
    left = lax.broadcasted_iota(jnp.int32, rope.shape, 1) < CODE
    for head in range(keys.shape[1] // (2 * NOPE)):
        at = head * 2 * NOPE
        first, second = keys[:, at : at + NOPE], keys[:, at + NOPE : at + 2 * NOPE]
        if head % 2 == 0:
            second = jnp.where(left, rope, code)
        else:
            first = jnp.where(left, code, first)
            second = jnp.where(left, second, rope)
        key_ref[:, at : at + NOPE] = first
        key_ref[:, at + NOPE : at + 2 * NOPE] = second


def lift(latent_rows, code, key_up, value_up):
    rows = latent_rows.shape[0]
    key_cols, value_cols = key_up.shape[1], value_up.shape[1]
    tiled = lambda cols: pl.BlockSpec((TILE, cols), lambda i: (i, 0))
    whole = lambda a: pl.BlockSpec(a.shape, lambda i: (0, 0))
    return pl.pallas_call(
        lift_kernel,
        grid=(rows // TILE,),
        in_specs=[tiled(WIDE), tiled(2 * CODE), whole(key_up), whole(value_up)],
        out_specs=[tiled(key_cols), tiled(value_cols)],
        out_shape=[
            jax.ShapeDtypeStruct((rows, key_cols), jnp.bfloat16),
            jax.ShapeDtypeStruct((rows, value_cols), jnp.bfloat16),
        ],
        compiler_params=pltpu.CompilerParams(vmem_limit_bytes=60 * MIB),
        cost_estimate=pl.CostEstimate(
            flops=2 * rows * LATENT * (key_cols + value_cols),
            bytes_accessed=2 * rows * (key_cols + value_cols + 768),
            transcendentals=0,
        ),
        name="lift",
    )(latent_rows, code, key_up, value_up)


def attend_kernel(
    first_ref, query_hbm, code_ref, key_prev, value_prev, key_own, value_own, out_hbm,
    query_ref, key_ref, value_ref, out_ref, key_sems, value_sems, query_sems, out_sems,
):
    tiles = query_ref.shape[0] // TILE
    heads = value_ref.shape[1] // VDIM
    to_log2 = math.log2(math.e) / math.sqrt(HEAD)
    first_tile = first_ref[0]

    def tile_rows(tile):
        return pl.ds(pl.multiple_of(tile * TILE, TILE), TILE)

    def key_copies(tile):
        here = tile_rows(tile)
        if tile < tiles:
            sources = (key_prev.at[here], value_prev.at[here])
        else:
            there = tile_rows(tile - tiles)
            sources = (key_own.at[there], value_own.at[there])
        return (
            pltpu.make_async_copy(sources[0], key_ref.at[here], key_sems.at[tile]),
            pltpu.make_async_copy(sources[1], value_ref.at[here], value_sems.at[tile]),
        )

    def query_copy(tile):
        here = tile_rows(tile)
        return pltpu.make_async_copy(query_hbm.at[here], query_ref.at[here], query_sems.at[tile])

    def out_copy(tile):
        here = tile_rows(tile)
        return pltpu.make_async_copy(out_ref.at[here], out_hbm.at[here], out_sems.at[tile])

    def start_keys(tile):
        for copy in key_copies(tile):
            copy.start()

    def wait_keys(tile):
        for copy in key_copies(tile):
            copy.wait()

    query_copy(0).start()
    start_keys(tiles)
    for tile in reversed(range(tiles)):
        pl.when(first_tile <= tile)(functools.partial(start_keys, tile))
    for tile in range(1, tiles):
        query_copy(tile).start()
        start_keys(tiles + tile)

    left = lax.broadcasted_iota(jnp.int32, (TILE, 128), 1) < CODE
    causal = lax.broadcasted_iota(jnp.int32, (TILE, TILE), 1) <= lax.broadcasted_iota(
        jnp.int32, (TILE, TILE), 0
    )

    def score(head, rows, span, code):
        at = head // 2 * PAIR
        middle = query_ref[rows, at + 128 : at + 256]
        if head % 2 == 0:
            query = [query_ref[rows, at : at + 128], jnp.where(left, middle, code)]
        else:
            query = [jnp.where(left, code, middle), query_ref[rows, at + 256 : at + 384]]
        return lax.dot_general(
            jnp.concatenate(query, axis=1),
            key_ref[span, head * 256 : (head + 1) * 256],
            (((1,), (1,)), ((), ())),
            preferred_element_type=jnp.float32,
        )

    def weigh(scores):
        far = scores.shape[1] - TILE
        own = jnp.where(causal, scores[:, far:], FAR)
        scores = jnp.concatenate([scores[:, :far], own], axis=1) if far else own
        top = jnp.max(scores, axis=1, keepdims=True) * to_log2
        return jnp.exp2(scores * to_log2 - top).astype(jnp.bfloat16)

    def attend_rows(step, count):
        rows = tile_rows(step)
        span = pl.ds(pl.multiple_of((tiles + 1 + step - count) * TILE, TILE), count * TILE)
        code = code_ref[rows, :]
        scores = [score(head, rows, span, code) for head in range(heads)]
        weights = [weigh(s) for s in scores]
        for head in range(heads):
            cols = slice(head * VDIM, (head + 1) * VDIM)
            ones = jnp.ones((count * TILE, VDIM), jnp.bfloat16)
            values = jnp.concatenate([value_ref[span, cols], ones], axis=1)
            total = jnp.dot(weights[head], values, preferred_element_type=jnp.float32)
            out_ref[rows, cols] = (total[:, :VDIM] / total[:, VDIM:]).astype(jnp.bfloat16)

    @pl.loop(0, tiles)
    def _(step):
        @pl.when(step == 0)
        def _():
            for tile in reversed(range(tiles)):
                pl.when(first_tile <= tile)(functools.partial(wait_keys, tile))

        for tile in range(tiles):

            @pl.when(step == tile)
            def _():
                query_copy(tile).wait()
                wait_keys(tiles + tile)

        count = tiles + 1 + step - first_ref[step]
        for n in range(1, tiles + 2):
            pl.when(count == n)(functools.partial(attend_rows, step, n))
        out_copy(step).start()

    for tile in range(tiles):
        out_copy(tile).wait()


def attend(first, query, code, key_prev, value_prev, key_own, value_own):
    rows, key_cols = key_own.shape
    value_cols = value_own.shape[1]
    tiles = rows // TILE
    vmem = pl.BlockSpec(memory_space=pltpu.VMEM)
    there = pl.BlockSpec(memory_space=pl.ANY)
    scratch = lambda r, c: pltpu.VMEM((r, c), jnp.bfloat16)
    return pl.pallas_call(
        attend_kernel,
        in_specs=[pl.BlockSpec(memory_space=pltpu.SMEM), there, vmem, there, there, there, there],
        out_specs=there,
        out_shape=jax.ShapeDtypeStruct((rows, value_cols), jnp.bfloat16),
        scratch_shapes=[
            scratch(rows, query.shape[1]),
            scratch(2 * rows, key_cols),
            scratch(2 * rows, value_cols),
            scratch(rows, value_cols),
            pltpu.SemaphoreType.DMA((2 * tiles,)),
            pltpu.SemaphoreType.DMA((2 * tiles,)),
            pltpu.SemaphoreType.DMA((tiles,)),
            pltpu.SemaphoreType.DMA((tiles,)),
        ],
        compiler_params=pltpu.CompilerParams(vmem_limit_bytes=60 * MIB),
        cost_estimate=pl.CostEstimate(
            flops=8 * rows * rows * key_cols,
            bytes_accessed=2 * rows * (2 * key_cols + 4 * value_cols),
            transcendentals=rows * rows * 4,
        ),
        name="attend",
    )(first, query, code, key_prev, value_prev, key_own, value_own)


def per_device(queries, latent, key_up, value_up, doc_lengths):
    uly_count = lax.axis_size("uly")
    own_rows = queries.shape[0]
    block_rows = own_rows * uly_count
    heads_dev = key_up.shape[1] // NOPE
    block_start = lax.axis_index("ctx") * block_rows
    pads = [(0, NOPE) if head % 2 == 0 else (CODE, ROPE) for head in range(heads_dev)]
    wide_up = jnp.concatenate(
        [jnp.pad(key_up[:, h * NOPE : (h + 1) * NOPE], ((0, 0), pads[h])) for h in range(heads_dev)],
        axis=1,
    )
    query_code, key_code = doc_codes(doc_lengths, block_start - block_rows, 2 * block_rows)
    first = first_tiles(doc_lengths, block_start, block_rows)

    own = lax.all_to_all(spread(latent, uly_count), "uly", split_axis=0, concat_axis=0)
    own = own.reshape(block_rows, WIDE)
    previous = passed_along(own, "ctx", 1)
    local_query = lax.all_to_all(queries, "uly", split_axis=1, concat_axis=0, tiled=True)
    key_own, value_own = lift(own, key_code[block_rows:], wide_up, value_up)
    key_prev, value_prev = lift(previous, key_code[:block_rows], wide_up, value_up)
    result = attend(
        first, local_query, query_code[block_rows:], key_prev, value_prev, key_own, value_own
    )
    result = result.reshape(uly_count, own_rows, heads_dev * VDIM)
    result = lax.all_to_all(result, "uly", split_axis=0, concat_axis=0)
    return jnp.transpose(result, (1, 0, 2)).reshape(own_rows, uly_count * heads_dev * VDIM)


def solution(mesh):
    placed = (P(("ctx", "uly"), None), P(("ctx", "uly"), None), P(None, "uly"), P(None, "uly"), P())
    return jax.shard_map(
        per_device, mesh=mesh, in_specs=placed, out_specs=P(("ctx", "uly"), None), check_vma=False
    )
```

time: 108 us -> 95.4 us (0.88)
  the two profiles are of different devices: /device:TPU:96 before, /device:TPU:225 now
where the time goes in v2:
time: 95.4 us; the launch traced here: 94.8 us
  blocking collectives  24.5 us (26%)
  Pallas kernels  21.6 us (23%)
  starting transfers between devices  18.9 us (20%)
  waiting for transfers between devices  12.9 us (14%)
  other arithmetic  11.3 us (12%)
  local copies, waits for them, and re-layouts  5.34 us (6%)
    all_to_all x1, blocking collectives, per_device(): result = lax.all_to_all(result, 'uly', split_axis=0, concat_axis=0)  24.5 us
    pallas_call x2, Pallas kernels, lift(): pl.pallas_call(lift_kernel, grid=(rows // TILE,), in_specs=[tiled(WIDE),...  10.4 us
    all_to_all x1, waiting for transfers between devices, per_device(): lax.all_to_all(spread(latent, uly_count), 'uly', split_axis=0, concat_axi...  9.81 us
    pallas_call x1, Pallas kernels, attend(): pl.pallas_call(attend_kernel, in_specs=[pl.BlockSpec(memory_space=pltpu.S...  8.91 us
    ppermute x1, starting transfers between devices, passed_along(): return lax.ppermute(block, axis, route)  7.49 us
    all_to_all x1, starting transfers between devices, per_device(): lax.all_to_all(spread(latent, uly_count), 'uly', split_axis=0, concat_axi...  6.77 us
    all_to_all x1, starting transfers between devices, per_device(): lax.all_to_all(queries, 'uly', split_axis=1, concat_axis=0, tiled=True)  4.66 us
    ppermute x1, waiting for transfers between devices, passed_along(): return lax.ppermute(block, axis, route)  3.14 us
  transfers between devices with their start and end apart: 3, of which 2 were waited for; matrix products, arithmetic and copies ran while one was open for 15% of the time, Pallas kernels for 11%

profile of v2, /device:TPU:225, one launch (start us, length us, event | category | flops | bytes accessed | tf_op | source)
XLA Modules:
  0.0 94.8 jit_solution(3807498398603525671)
XLA Ops:
  0.0 2.3 %spread.1 = bf16[16,64,640]{2,1,0:T(8,128)(2,1)} custom-call(bf16[64,576]{1,0:T(8,128)(2,1)} %latent_ref.1), custom_call_target="tpu_custom_call" | custom-call | tf_op jit(solution)/shard_map/spread/pallas_call | solution.py:67
  2.3 6.8 %all-to-all-start.1 = ((bf16[16,64,640]{2,1,0:T(8,128)(2,1)}), bf16[16,64,640]{2,1,0:T(8,128)(2,1)S(1)}, u32[]{:S(2)}, u32[]{:S(2)}) async-start(bf16[16,64,640]{2,1,0:T(8,128)(2,1)} %spread.1), calls=%async_computation.1 | async-start | bytes 2621440 | tf_op jit(solution)/shard_map/all_to_all | solution.py:277
  9.1 0.0 copy-start.3
  9.1 0.6 broadcast_compare_fusion
  9.7 0.5 multiply_add_fusion
  10.2 0.1 copy.12
  10.3 0.2 reduce-window.8
  10.5 0.1 reduce
  10.6 0.7 sub.23
  11.3 0.6 convert_reduce_fusion
  12.0 0.0 copy-start.4
  12.0 0.0 copy-start.9
  12.0 1.3 %copy.18 = bf16[8,16,8,768]{3,2,0,1:T(8,128)(2,1)} copy(bf16[8,16,8,768]{3,2,1,0:T(8,128)(2,1)S(1)} %bitcast.14) | data formatting | bytes 3145728 | tf_op jit(solution)/shard_map/all_to_all | solution.py:280
  13.3 0.7 select_reduce_fusion
  14.1 0.5 and_or_fusion
  14.6 1.2 %compare_or_fusion = pred[2048,128]{1,0:T(8,128)(4,1)S(1)} fusion(s32[128]{0:T(128)S(1)} %and_select_fusion, s32[2048]{0:T(1024)S(1)} %get-tuple-element.19, s32[2048]{0:T(1024)S(1)} %get-tuple-element.18), kind=kLoop, calls=%fused_computation.16 | loop fusion | flops 786432 | bytes 279040 | tf_op jit(solution)/shard_map/or | solution.py:36
  15.8 0.8 select_convert_fusion.1.code_ref
  16.6 0.8 fusion.12
  17.4 9.8 %all-to-all-done.1 = bf16[16,64,640]{2,1,0:T(8,128)(2,1)S(1)} async-done(((bf16[16,64,640]{2,1,0:T(8,128)(2,1)}), bf16[16,64,640]{2,1,0:T(8,128)(2,1)S(1)}, u32[]{:S(2)}, u32[]{:S(2)}) %all-to-all-start.1) | async-done | bytes 1310752 | tf_op jit(solution)/shard_map/all_to_all | solution.py:277
  27.2 4.7 %all-to-all-start = ((bf16[64,16,768]{2,0,1:T(8,128)(2,1)}), bf16[64,16,768]{2,0,1:T(8,128)(2,1)S(1)}, u32[]{:S(2)}, u32[]{:S(2)}) async-start(bf16[64,16,768]{2,0,1:T(8,128)(2,1)} %bitcast.12), calls=%async_computation | async-start | bytes 3145728 | tf_op jit(solution)/shard_map/all_to_all | solution.py:280
  31.8 7.5 %collective-permute-start = (bf16[1024,640]{1,0:T(8,128)(2,1)S(1)}, bf16[1024,640]{1,0:T(8,128)(2,1)}, u32[]{:S(2)}, u32[]{:S(2)}) collective-permute-start(bf16[1024,640]{1,0:T(8,128)(2,1)S(1)} %bitcast.16), channel_id=1, source_target_pairs={{0,16},{16,32},{32,48},{48,64},{64,80},{80,96},{96,112},{112,128},... | collective-permute-start | bytes 3932168 | tf_op jit(solution)/shard_map/ppermute | solution.py:27
  39.3 1.2 %and_select_fusion.1.first_ref = s32[4]{0:T(128)} fusion(s32[4]{0:T(128)} %select_reduce_fusion, s32[]{:T(128)S(6)} %sub.24), kind=kLoop, calls=%fused_computation.33 | loop fusion | flops 64 | bytes 36 | tf_op jit(solution)/shard_map/jit(floor_divide)/jit(_where)/select_n | solution.py:49
  40.5 2.9 %select_convert_fusion = bf16[2048,128]{1,0:T(8,128)(2,1)S(1)} fusion(pred[2048]{0:T(1024)(128)(4,1)} %broadcast_compare_fusion, pred[128]{0:T(512)(128)(4,1)} %and_or_fusion, s32[2048]{0:T(1024)S(1)} %get-tuple-element.19, s32[2048]{0:T(1024)S(1)} %get-tuple-element.18, s32[128]{0:T(128)} %copy-done.7), kind=kLoop, calls=%fused_computation.14 | loop fusion | flops 2097152 | bytes 543360 | tf_op jit(solution)/shard_map/convert_element_type | solution.py:40
  43.5 0.8 fusion.11
  44.3 1.2 %fusion.6.key_up_ref = bf16[512,1024]{1,0:T(8,128)(2,1)} fusion(bf16[512,128]{1,0:T(8,128)(2,1)S(1)} %copy-done.5, bf16[512,128]{1,0:T(8,128)(2,1)S(1)} %copy-done.6, bf16[512,128]{1,0:T(8,128)(2,1)S(1)} %get-tuple-element.15, bf16[512,256]{1,0:T(8,128)(2,1)S(1)} %slice_select_fusion), kind=kLoop, calls=%fused_computation.12 | loop fusion | flops 9437184 | bytes 1703936 | tf_op jit(solution)/shard_map/concatenate | solution.py:270
  45.6 5.2 %lift.3 = (bf16[1024,1024]{1,0:T(8,128)(2,1)}, bf16[1024,512]{1,0:T(8,128)(2,1)}) custom-call(bf16[1024,640]{1,0:T(8,128)(2,1)} %bitcast.17, bf16[1024,128]{1,0:T(8,128)(2,1)} %get-tuple-element.13.code_ref, bf16[512,1024]{1,0:T(8,128)(2,1)} %fusion.6.key_up_ref, bf16[512,512]{1,0:T(8,128)(2,1)} %value_up_ref.3), custom_call_target="tpu_custom_call" | custom-call | flops 1610612736 | bytes 4718592 | tf_op jit(solution)/shard_map/lift/pallas_call | solution.py:102
  50.7 3.1 %collective-permute-done.latent_ref = bf16[1024,640]{1,0:T(8,128)(2,1)} collective-permute-done((bf16[1024,640]{1,0:T(8,128)(2,1)S(1)}, bf16[1024,640]{1,0:T(8,128)(2,1)}, u32[]{:S(2)}, u32[]{:S(2)}) %collective-permute-start) | collective-permute-done | bytes 1310752 | tf_op jit(solution)/shard_map/ppermute | solution.py:27
  53.9 5.2 %lift.2 = (bf16[1024,1024]{1,0:T(8,128)(2,1)}, bf16[1024,512]{1,0:T(8,128)(2,1)}) custom-call(bf16[1024,640]{1,0:T(8,128)(2,1)} %collective-permute-done.latent_ref, bf16[1024,128]{1,0:T(8,128)(2,1)} %get-tuple-element.14.code_ref, bf16[512,1024]{1,0:T(8,128)(2,1)} %fusion.6.key_up_ref, bf16[512,512]{1,0:T(8,128)(2,1)} %value_up_ref.3), custom_call_target="tpu_custom_call" | custom-call | flops 1610612736 | bytes 4718592 | tf_op jit(solution)/shard_map/lift/pallas_call | solution.py:102
  59.1 1.2 %copy-done.1 = bf16[64,16,768]{2,0,1:T(8,128)(2,1)} copy-done((bf16[64,16,768]{2,0,1:T(8,128)(2,1)}, bf16[64,16,768]{2,0,1:T(8,128)(2,1)S(1)}, u32[]{:S(2)}) %copy-start.1) | copy-done | bytes 1572888
  60.3 8.9 %attend.1 = bf16[1024,512]{1,0:T(8,128)(2,1)} custom-call(s32[4]{0:T(128)} %and_select_fusion.1.first_ref, bf16[1024,768]{1,0:T(8,128)(2,1)} %bitcast.15, bf16[1024,128]{1,0:T(8,128)(2,1)} %select_convert_fusion.1.code_ref, bf16[1024,1024]{1,0:T(8,128)(2,1)} %get-tuple-element.9.key_prev, bf16[1024,512]{1,0:T(8,128)(2,1)} %get-tuple-element.10.value_prev, ...), custom_call_target="tpu_custom_call" | custom-call | flops 8589934592 | bytes 8388608 | tf_op jit(solution)/shard_map/attend/pallas_call | solution.py:238
  69.2 24.5 %all_to_all.29 = bf16[16,64,512]{2,1,0:T(8,128)(2,1)S(1)} all-to-all(bf16[16,64,512]{2,1,0:T(8,128)(2,1)} %bitcast.18), channel_id=1, replica_groups=mesh['ctx'=32,'uly'=16] {'uly'}, dimensions={0} | all-to-all | bytes 2097152 | tf_op jit(solution)/shard_map/all_to_all | solution.py:287
  93.7 1.1 %copy.16 = bf16[16,8,8,512]{3,2,0,1:T(8,128)(2,1)} copy(bf16[16,8,8,512]{3,2,1,0:T(8,128)(2,1)S(1)} %bitcast.13) | data formatting | bytes 2097152 | tf_op jit(solution)/shard_map/reshape | solution.py:288
  (23 shorter events, 0.1 us)
Async XLA Ops:
  0.0 10.2 %copy-start.8 = (s32[128]{0:T(128)S(1)}, s32[128]{0:T(128)}, u32[]{:S(2)}) copy-start(s32[128]{0:T(128)} %param.9) | copy-start | bytes 1540
  0.0 12.0 %copy-start = (bf16[64,12288]{1,0:T(8,128)(2,1)S(1)}, bf16[64,12288]{1,0:T(8,128)(2,1)}, u32[]{:S(2)}) copy-start(bf16[64,12288]{1,0:T(8,128)(2,1)} %param.5) | copy-start | bytes 4718596
  2.3 24.9 %all-to-all-start.1 = ((bf16[16,64,640]{2,1,0:T(8,128)(2,1)}), bf16[16,64,640]{2,1,0:T(8,128)(2,1)S(1)}, u32[]{:S(2)}, u32[]{:S(2)}) async-start(bf16[16,64,640]{2,1,0:T(8,128)(2,1)} %spread.1), calls=%async_computation.1 | async-start | bytes 2621440 | tf_op jit(solution)/shard_map/all_to_all | solution.py:277
  9.1 7.5 %copy-start.3 = (bf16[512,512]{1,0:T(8,128)(2,1)S(1)}, bf16[512,512]{1,0:T(8,128)(2,1)}, u32[]{:S(2)}) copy-start(bf16[512,512]{1,0:T(8,128)(2,1)} %param.7) | copy-start | bytes 1572868
  9.7 7.6 %copy-start.7 = (s32[128]{0:T(128)}, s32[128]{0:T(128)S(1)}, u32[]{:S(2)}) copy-start(s32[128]{0:T(128)S(1)} %and_select_fusion) | copy-start | bytes 1540
  10.5 2.8 %copy-start.10 = (s32[4]{0:T(128)S(1)}, s32[4]{0:T(128)}, u32[]{:S(2)}) copy-start(s32[4]{0:T(128)} %multiply_add_fusion) | copy-start | bytes 52
  12.0 5.4 %copy-start.4 = (bf16[512,512]{1,0:T(8,128)(2,1)S(1)}, bf16[512,512]{1,0:T(8,128)(2,1)}, u32[]{:S(2)}) copy-start(bf16[512,512]{1,0:T(8,128)(2,1)} %param.7) | copy-start | bytes 1572868
  12.0 5.4 %copy-start.9 = (pred[256]{0:T(512)(128)(4,1)S(1)}, pred[256]{0:T(512)(128)(4,1)}, u32[]{:S(2)}) copy-start(pred[256]{0:T(512)(128)(4,1)} %constant.90.clone.1) | copy-start | bytes 772
  27.2 17.1 %copy-start.2 = (bf16[16,64,640]{2,1,0:T(8,128)(2,1)}, bf16[16,64,640]{2,1,0:T(8,128)(2,1)S(1)}, u32[]{:S(2)}) copy-start(bf16[16,64,640]{2,1,0:T(8,128)(2,1)S(1)} %all-to-all-done.1) | copy-start | bytes 3932164
  27.2 17.1 %copy-start.5 = (bf16[512,128]{1,0:T(8,128)(2,1)S(1)}, bf16[512,128]{1,0:T(8,128)(2,1)}, u32[]{:S(2)}) copy-start(bf16[512,128]{1,0:T(8,128)(2,1)} %get-tuple-element.16) | copy-start | bytes 393220
  27.2 17.2 %copy-start.6 = (bf16[512,128]{1,0:T(8,128)(2,1)S(1)}, bf16[512,128]{1,0:T(8,128)(2,1)}, u32[]{:S(2)}) copy-start(bf16[512,128]{1,0:T(8,128)(2,1)} %get-tuple-element.17) | copy-start | bytes 393220
  27.2 31.9 %all-to-all-start = ((bf16[64,16,768]{2,0,1:T(8,128)(2,1)}), bf16[64,16,768]{2,0,1:T(8,128)(2,1)S(1)}, u32[]{:S(2)}, u32[]{:S(2)}) async-start(bf16[64,16,768]{2,0,1:T(8,128)(2,1)} %bitcast.12), calls=%async_computation | async-start | bytes 3145728 | tf_op jit(solution)/shard_map/all_to_all | solution.py:280
  31.8 22.0 %collective-permute-start = (bf16[1024,640]{1,0:T(8,128)(2,1)S(1)}, bf16[1024,640]{1,0:T(8,128)(2,1)}, u32[]{:S(2)}, u32[]{:S(2)}) collective-permute-start(bf16[1024,640]{1,0:T(8,128)(2,1)S(1)} %bitcast.16), channel_id=1, source_target_pairs={{0,16},{16,32},{32,48},{48,64},{64,80},{80,96},{96,112},{112,128},... | collective-permute-start | bytes 3932168 | tf_op jit(solution)/shard_map/ppermute | solution.py:27
  59.1 1.2 %copy-start.1 = (bf16[64,16,768]{2,0,1:T(8,128)(2,1)}, bf16[64,16,768]{2,0,1:T(8,128)(2,1)S(1)}, u32[]{:S(2)}) copy-start(bf16[64,16,768]{2,0,1:T(8,128)(2,1)S(1)} %all-to-all-done) | copy-start | bytes 4718596

commit v3 on v2

v3 whole, which is shorter than its diff:
```python
import functools
import math

import jax
import jax.numpy as jnp
from jax import lax
from jax.experimental import pallas as pl
from jax.experimental.pallas import tpu as pltpu
from jax.sharding import PartitionSpec as P

LATENT = 512
ROPE = 64
NOPE = 128
VDIM = 128
HEAD = NOPE + ROPE
PAIR = 2 * HEAD
CHUNKS = LATENT // 128
TILE = 256
CODE = 64
FAR = -(2.0**40)
MIB = 1 << 20


def passed_along(block, axis, distance):
    devices = range(lax.axis_size(axis))
    route = [(i - distance, i) for i in devices if i - distance in devices]
    return lax.ppermute(block, axis, route)


def doc_codes(doc_lengths, first, rows):
    position = first + jnp.arange(rows, dtype=jnp.int32)
    ends = jnp.cumsum(doc_lengths)
    doc = jnp.sum((ends[None, :] <= position[:, None]).astype(jnp.int32), axis=1)
    high, low = doc // 8, doc % 8
    lane = (jnp.arange(2 * CODE, dtype=jnp.int32) % CODE)[None, :]
    hot = (lane == high[:, None]) | (lane == 32 + low[:, None])
    used = (lane < 16) | ((lane >= 32) & (lane < 40))
    inside = (position >= 0)[:, None]
    query_code = jnp.where(hot, 1.0, 0.0).astype(jnp.bfloat16)
    key_code = jnp.where(used & ~(hot & inside), FAR, 0.0).astype(jnp.bfloat16)
    return query_code, key_code


def first_tiles(doc_lengths, block_start, block_rows):
    starts = jnp.cumsum(doc_lengths) - doc_lengths
    position = block_start + TILE * jnp.arange(block_rows // TILE, dtype=jnp.int32)
    before = starts[None, :] <= position[:, None]
    first_key = jnp.max(jnp.where(before, starts[None, :], 0), axis=1)
    return (first_key - (block_start - block_rows)) // TILE


def spread_kernel(latent_ref, copies_ref):
    rows = latent_ref.shape[0]
    half = rows // 2
    rope = latent_ref[:, LATENT:]
    chunks = [latent_ref[:, i * 128 : (i + 1) * 128] for i in range(CHUNKS)]
    packed = jnp.concatenate(chunks + [jnp.concatenate([rope[:half], rope[half:]], axis=1)], axis=0)
    for i in range(copies_ref.shape[0]):
        copies_ref[i] = packed


def spread(latent, count):
    rows = latent.shape[0]
    vmem = pl.BlockSpec(memory_space=pltpu.VMEM)
    return pl.pallas_call(
        spread_kernel,
        in_specs=[vmem],
        out_specs=vmem,
        out_shape=jax.ShapeDtypeStruct((count, rows * CHUNKS + rows // 2, 128), latent.dtype),
        compiler_params=pltpu.CompilerParams(vmem_limit_bytes=16 * MIB),
        name="spread",
    )(latent)


def lift_tile(packed, code, key_up, value_up):
    count, rows = packed.shape[0], packed.shape[1] * 2 // (2 * CHUNKS + 1)
    chunks = [
        packed[:, i * rows : (i + 1) * rows].reshape(count * rows, 128) for i in range(CHUNKS)
    ]
    compact = jnp.concatenate(chunks, axis=1)
    ropes = packed[:, CHUNKS * rows :].reshape(count * rows // 2, 128)
    low = lax.broadcasted_iota(jnp.int32, ropes.shape, 1) < ROPE
    other = jnp.concatenate([ropes[:, ROPE:], ropes[:, :ROPE]], axis=1)
    firsts = jnp.where(low, ropes, other).reshape(count, rows // 2, 128)
    seconds = jnp.where(low, other, ropes).reshape(count, rows // 2, 128)
    rope = jnp.concatenate([firsts, seconds], axis=1).reshape(count * rows, 128)
    keys = jnp.dot(compact, key_up, preferred_element_type=jnp.float32).astype(jnp.bfloat16)
    values = jnp.dot(compact, value_up, preferred_element_type=jnp.float32).astype(jnp.bfloat16)
    left = lax.broadcasted_iota(jnp.int32, rope.shape, 1) < CODE
    columns = []
    for head in range(keys.shape[1] // NOPE):
        key = keys[:, head * NOPE : (head + 1) * NOPE]
        if head % 2 == 0:
            columns += [key, jnp.where(left, rope, code)]
        else:
            turned = jnp.concatenate([key[:, CODE:], key[:, :CODE]], axis=1)
            columns += [jnp.where(left, code, turned), jnp.where(left, turned, rope)]
    return columns, values


def lift_kernel(packed_ref, code_ref, key_up_ref, value_up_ref, key_ref, value_ref):
    columns, values = lift_tile(packed_ref[...], code_ref[...], key_up_ref[...], value_up_ref[...])
    for i, column in enumerate(columns):
        key_ref[:, i * 128 : (i + 1) * 128] = column
    value_ref[...] = values


def lift(packed, code, key_up, value_up):
    rows = code.shape[0]
    steps = rows // TILE
    key_cols, value_cols = 2 * key_up.shape[1], value_up.shape[1]
    tiled = lambda cols: pl.BlockSpec((TILE, cols), lambda i: (i, 0))
    whole = lambda a: pl.BlockSpec(a.shape, lambda i: (0, 0))
    packed_spec = pl.BlockSpec((packed.shape[0] // steps,) + packed.shape[1:], lambda i: (i, 0, 0))
    return pl.pallas_call(
        lift_kernel,
        grid=(steps,),
        in_specs=[packed_spec, tiled(2 * CODE), whole(key_up), whole(value_up)],
        out_specs=[tiled(key_cols), tiled(value_cols)],
        out_shape=[
            jax.ShapeDtypeStruct((rows, key_cols), jnp.bfloat16),
            jax.ShapeDtypeStruct((rows, value_cols), jnp.bfloat16),
        ],
        compiler_params=pltpu.CompilerParams(vmem_limit_bytes=60 * MIB),
        cost_estimate=pl.CostEstimate(
            flops=2 * rows * LATENT * (key_cols + value_cols),
            bytes_accessed=2 * rows * (key_cols + value_cols + 768),
            transcendentals=0,
        ),
        name="lift",
    )(packed, code, key_up, value_up)


def attend_kernel(
    first_ref, query_hbm, code_hbm, prev_hbm, prev_code_hbm, key_up_hbm, value_up_hbm, key_own,
    value_own, out_hbm, query_ref, code_ref, prev_ref, prev_code_ref, key_up_ref, value_up_ref,
    key_ref, value_ref, out_ref, key_sems, value_sems, query_sems, out_sems, lift_sems, prev_sems,
    code_sem,
):
    tiles = query_ref.shape[0] // TILE
    heads = value_ref.shape[1] // VDIM
    to_log2 = math.log2(math.e) / math.sqrt(HEAD)
    first_tile = first_ref[0]

    def tile_rows(tile):
        return pl.ds(pl.multiple_of(tile * TILE, TILE), TILE)

    def key_copies(tile):
        here, there = tile_rows(tile), tile_rows(tiles + tile)
        return (
            pltpu.make_async_copy(key_own.at[here], key_ref.at[there], key_sems.at[tile]),
            pltpu.make_async_copy(value_own.at[here], value_ref.at[there], value_sems.at[tile]),
        )

    def query_copy(tile):
        here = tile_rows(tile)
        return pltpu.make_async_copy(query_hbm.at[here], query_ref.at[here], query_sems.at[tile])

    def out_copy(tile):
        here = tile_rows(tile)
        return pltpu.make_async_copy(out_ref.at[here], out_hbm.at[here], out_sems.at[tile])

    share = prev_ref.shape[0] // tiles

    def prev_copy(tile):
        here = pl.ds(tile * share, share)
        return pltpu.make_async_copy(prev_hbm.at[here], prev_ref.at[here], prev_sems.at[tile])

    lift_copies = [
        pltpu.make_async_copy(source, target, lift_sems.at[i])
        for i, (source, target) in enumerate(
            [(key_up_hbm, key_up_ref), (value_up_hbm, value_up_ref), (prev_code_hbm, prev_code_ref)]
        )
    ]
    code_copy = pltpu.make_async_copy(code_hbm, code_ref, code_sem)

    @pl.when(first_tile < tiles)
    def _():
        for copy in lift_copies:
            copy.start()
        for tile in range(tiles):
            pl.when(first_tile <= tile)(lambda tile=tile: prev_copy(tile).start())

    code_copy.start()
    for tile in range(tiles):
        query_copy(tile).start()
        for copy in key_copies(tile):
            copy.start()

    @pl.when(first_tile < tiles)
    def _():
        for copy in lift_copies:
            copy.wait()

    @pl.loop(jnp.minimum(first_tile, tiles), tiles)
    def _(tile):
        prev_copy(tile).wait()
        rows = tile_rows(tile)
        packed = prev_ref[pl.ds(tile * share, share)]
        columns, values = lift_tile(packed, prev_code_ref[rows, :], key_up_ref[...], value_up_ref[...])
        for i, column in enumerate(columns):
            key_ref[rows, i * 128 : (i + 1) * 128] = column
        value_ref[rows, :] = values

    left = lax.broadcasted_iota(jnp.int32, (TILE, 128), 1) < CODE
    causal = lax.broadcasted_iota(jnp.int32, (TILE, TILE), 1) <= lax.broadcasted_iota(
        jnp.int32, (TILE, TILE), 0
    )

    def score(head, rows, span, code):
        at = head // 2 * PAIR
        middle = query_ref[rows, at + 128 : at + 256]
        if head % 2 == 0:
            query = [query_ref[rows, at : at + 128], jnp.where(left, middle, code)]
        else:
            query = [jnp.where(left, code, middle), query_ref[rows, at + 256 : at + 384]]
        return lax.dot_general(
            jnp.concatenate(query, axis=1),
            key_ref[span, head * 256 : (head + 1) * 256],
            (((1,), (1,)), ((), ())),
            preferred_element_type=jnp.float32,
        )

    def weigh(scores):
        far = scores.shape[1] - TILE
        own = jnp.where(causal, scores[:, far:], FAR)
        scores = jnp.concatenate([scores[:, :far], own], axis=1) if far else own
        top = jnp.max(scores, axis=1, keepdims=True) * to_log2
        return jnp.exp2(scores * to_log2 - top).astype(jnp.bfloat16)

    def attend_rows(step, count):
        rows = tile_rows(step)
        span = pl.ds(pl.multiple_of((tiles + 1 + step - count) * TILE, TILE), count * TILE)
        code = code_ref[rows, :]
        scores = [score(head, rows, span, code) for head in range(heads)]
        weights = [weigh(s) for s in scores]
        for head in range(heads):
            cols = slice(head * VDIM, (head + 1) * VDIM)
            ones = jnp.ones((count * TILE, VDIM), jnp.bfloat16)
            values = jnp.concatenate([value_ref[span, cols], ones], axis=1)
            total = jnp.dot(weights[head], values, preferred_element_type=jnp.float32)
            out_ref[rows, cols] = (total[:, :VDIM] / total[:, VDIM:]).astype(jnp.bfloat16)

    code_copy.wait()

    @pl.loop(0, tiles)
    def _(step):
        for tile in range(tiles):

            @pl.when(step == tile)
            def _():
                query_copy(tile).wait()
                for copy in key_copies(tile):
                    copy.wait()

        count = tiles + 1 + step - first_ref[step]
        for n in range(1, tiles + 2):
            pl.when(count == n)(functools.partial(attend_rows, step, n))
        out_copy(step).start()

    for tile in range(tiles):
        out_copy(tile).wait()


def attend(first, query, code, prev, prev_code, key_up, value_up, key_own, value_own):
    rows, key_cols = key_own.shape
    value_cols = value_own.shape[1]
    tiles = rows // TILE
    there = pl.BlockSpec(memory_space=pl.ANY)
    scratch = lambda *shape: pltpu.VMEM(shape, jnp.bfloat16)
    return pl.pallas_call(
        attend_kernel,
        in_specs=[pl.BlockSpec(memory_space=pltpu.SMEM)] + [there] * 8,
        out_specs=there,
        out_shape=jax.ShapeDtypeStruct((rows, value_cols), jnp.bfloat16),
        scratch_shapes=[
            scratch(*query.shape),
            scratch(*code.shape),
            scratch(*prev.shape),
            scratch(*prev_code.shape),
            scratch(*key_up.shape),
            scratch(*value_up.shape),
            scratch(2 * rows, key_cols),
            scratch(2 * rows, value_cols),
            scratch(rows, value_cols),
            pltpu.SemaphoreType.DMA((tiles,)),
            pltpu.SemaphoreType.DMA((tiles,)),
            pltpu.SemaphoreType.DMA((tiles,)),
            pltpu.SemaphoreType.DMA((tiles,)),
            pltpu.SemaphoreType.DMA((3,)),
            pltpu.SemaphoreType.DMA((tiles,)),
            pltpu.SemaphoreType.DMA,
        ],
        compiler_params=pltpu.CompilerParams(vmem_limit_bytes=60 * MIB),
        cost_estimate=pl.CostEstimate(
            flops=8 * rows * rows * key_cols,
            bytes_accessed=2 * rows * (2 * key_cols + 4 * value_cols),
            transcendentals=rows * rows * 4,
        ),
        name="attend",
    )(first, query, code, prev, prev_code, key_up, value_up, key_own, value_own)


def per_device(queries, latent, key_up, value_up, doc_lengths):
    uly_count = lax.axis_size("uly")
    own_rows = queries.shape[0]
    block_rows = own_rows * uly_count
    heads_dev = key_up.shape[1] // NOPE
    block_start = lax.axis_index("ctx") * block_rows
    query_code, key_code = doc_codes(doc_lengths, block_start - block_rows, 2 * block_rows)
    first = first_tiles(doc_lengths, block_start, block_rows)

    own = lax.all_to_all(spread(latent, uly_count), "uly", split_axis=0, concat_axis=0)
    previous = passed_along(own, "ctx", 1)
    local_query = lax.all_to_all(queries, "uly", split_axis=1, concat_axis=0, tiled=True)
    key_own, value_own = lift(own, key_code[block_rows:], key_up, value_up)
    result = attend(
        first, local_query, query_code[block_rows:], previous, key_code[:block_rows], key_up, value_up,
        key_own, value_own,
    )
    result = result.reshape(uly_count, own_rows, heads_dev * VDIM)
    result = lax.all_to_all(result, "uly", split_axis=0, concat_axis=0)
    return jnp.transpose(result, (1, 0, 2)).reshape(own_rows, uly_count * heads_dev * VDIM)


def solution(mesh):
    placed = (P(("ctx", "uly"), None), P(("ctx", "uly"), None), P(None, "uly"), P(None, "uly"), P())
    return jax.shard_map(
        per_device, mesh=mesh, in_specs=placed, out_specs=P(("ctx", "uly"), None), check_vma=False
    )
```

time: 95.4 us -> 87.9 us (0.921)
  the two profiles are of different devices: /device:TPU:225 before, /device:TPU:1 now
where the time goes in v3:
time: 87.9 us; the launch traced here: 87.4 us
  blocking collectives  22.1 us (25%)
  starting transfers between devices  19.4 us (22%)
  Pallas kernels  17.8 us (20%)
  waiting for transfers between devices  17.2 us (20%)
  other arithmetic  5.41 us (6%)
  local copies, waits for them, and re-layouts  5.37 us (6%)
    all_to_all x1, blocking collectives, per_device(): result = lax.all_to_all(result, 'uly', split_axis=0, concat_axis=0)  22.1 us
    all_to_all x1, waiting for transfers between devices, per_device(): lax.all_to_all(spread(latent, uly_count), 'uly', split_axis=0, concat_axi...  11.9 us
    pallas_call x1, Pallas kernels, attend(): pl.pallas_call(attend_kernel, in_specs=[pl.BlockSpec(memory_space=pltpu.S...  11.8 us
    all_to_all x1, starting transfers between devices, per_device(): lax.all_to_all(spread(latent, uly_count), 'uly', split_axis=0, concat_axi...  7.72 us
    ppermute x1, starting transfers between devices, passed_along(): return lax.ppermute(block, axis, route)  6.28 us
    all_to_all x1, starting transfers between devices, per_device(): lax.all_to_all(queries, 'uly', split_axis=1, concat_axis=0, tiled=True)  5.37 us
    all_to_all x1, waiting for transfers between devices, per_device(): lax.all_to_all(queries, 'uly', split_axis=1, concat_axis=0, tiled=True)  5.3 us
    pallas_call x1, Pallas kernels, lift(): pl.pallas_call(lift_kernel, grid=(steps,), in_specs=[packed_spec, tiled(2...  4.82 us
  transfers between devices with their start and end apart: 3, of which 2 were waited for; matrix products, arithmetic and copies ran while one was open for 9% of the time, Pallas kernels for 6%

profile of v3, /device:TPU:1, one launch (start us, length us, event | category | flops | bytes accessed | tf_op | source)
XLA Modules:
  0.0 87.4 jit_solution(14051052544141436589)
XLA Ops:
  0.0 0.0 copy-start
  0.0 0.9 %copy-done = bf16[64,576]{1,0:T(8,128)(2,1)S(1)} copy-done((bf16[64,576]{1,0:T(8,128)(2,1)S(1)}, bf16[64,576]{1,0:T(8,128)(2,1)}, u32[]{:S(2)}) %copy-start) | copy-done | bytes 73752
  0.9 0.0 copy-start.4
  0.9 1.2 %spread.1 = bf16[16,288,128]{2,1,0:T(8,128)(2,1)} custom-call(bf16[64,576]{1,0:T(8,128)(2,1)S(1)} %copy-done), custom_call_target="tpu_custom_call" | custom-call | tf_op jit(solution)/shard_map/spread/pallas_call | solution.py:65
  2.0 0.0 copy-start.1
  2.1 7.7 %all-to-all-start.1 = ((bf16[16,288,128]{2,1,0:T(8,128)(2,1)}), bf16[16,288,128]{2,1,0:T(8,128)(2,1)S(1)}, u32[]{:S(2)}, u32[]{:S(2)}) async-start(bf16[16,288,128]{2,1,0:T(8,128)(2,1)} %spread.1), calls=%async_computation.1 | async-start | bytes 2359296 | tf_op jit(solution)/shard_map/all_to_all | solution.py:313
  9.8 0.0 copy-done.4
  9.8 0.1 copy.12
  9.9 0.2 reduce-window.8
  10.1 0.1 reduce
  10.2 0.0 copy-done.1
  10.2 1.3 %copy.18 = bf16[8,16,8,768]{3,2,0,1:T(8,128)(2,1)} copy(bf16[8,16,8,768]{3,2,1,0:T(8,128)(2,1)S(1)} %bitcast.13) | data formatting | bytes 3145728 | tf_op jit(solution)/shard_map/all_to_all | solution.py:315
  11.5 0.2 select_reduce_fusion
  11.7 0.6 convert_reduce_fusion
  12.4 1.2 %compare_or_fusion = pred[2048,128]{1,0:T(8,128)(4,1)S(1)} fusion(s32[128]{0:T(128)S(1)} %and_select_fusion, s32[2048]{0:T(1024)S(1)} %get-tuple-element.12, s32[2048]{0:T(1024)S(1)} %get-tuple-element.11), kind=kLoop, calls=%fused_computation.3 | loop fusion | flops 786432 | bytes 279040 | tf_op jit(solution)/shard_map/or | solution.py:36
  13.6 11.9 %all-to-all-done.1.packed_ref = bf16[16,288,128]{2,1,0:T(8,128)(2,1)S(1)} async-done(((bf16[16,288,128]{2,1,0:T(8,128)(2,1)}), bf16[16,288,128]{2,1,0:T(8,128)(2,1)S(1)}, u32[]{:S(2)}, u32[]{:S(2)}) %all-to-all-start.1) | async-done | bytes 1179680 | tf_op jit(solution)/shard_map/all_to_all | solution.py:313
  25.5 0.0 copy-start.3
  25.5 5.4 %all-to-all-start = ((bf16[64,16,768]{2,0,1:T(8,128)(2,1)}), bf16[64,16,768]{2,0,1:T(8,128)(2,1)S(1)}, u32[]{:S(2)}, u32[]{:S(2)}) async-start(bf16[64,16,768]{2,0,1:T(8,128)(2,1)} %bitcast.11), calls=%async_computation | async-start | bytes 3145728 | tf_op jit(solution)/shard_map/all_to_all | solution.py:315
  30.9 0.6 and_select_fusion.1.first_ref
  31.5 0.0 copy-done.3
  31.5 6.3 %collective-permute-start = (bf16[16,288,128]{2,1,0:T(8,128)(2,1)S(1)}, bf16[16,288,128]{2,1,0:T(8,128)(2,1)}, u32[]{:S(2)}, u32[]{:S(2)}) collective-permute-start(bf16[16,288,128]{2,1,0:T(8,128)(2,1)S(1)} %all-to-all-done.1.packed_ref), channel_id=1, source_target_pairs={{0,16},{16,32},{32,48},{48,64},{64,80},{80,96},{96,112},{112,128},... | collective-permute-start | bytes 3538952 | tf_op jit(solution)/shard_map/ppermute | solution.py:27
  37.8 0.8 select_convert_fusion.1.code_hbm
  38.6 1.7 %select_convert_fusion = bf16[2048,128]{1,0:T(8,128)(2,1)S(1)} fusion(pred[2048]{0:T(1024)(128)(4,1)S(1)} %broadcast_compare_fusion, pred[128]{0:T(512)(128)(4,1)S(1)} %and_or_fusion, s32[2048]{0:T(1024)S(1)} %get-tuple-element.12, s32[2048]{0:T(1024)S(1)} %get-tuple-element.11, s32[128]{0:T(128)S(1)} %and_select_fusion), kind=kLoop, calls=%fused_computation.1 | loop fusion | flops 2097152 | bytes 543360 | tf_op jit(solution)/shard_map/convert_element_type | solution.py:40
  40.3 0.8 fusion.3
  41.1 4.8 %lift.1 = (bf16[1024,1024]{1,0:T(8,128)(2,1)}, bf16[1024,512]{1,0:T(8,128)(2,1)}) custom-call(bf16[16,288,128]{2,1,0:T(8,128)(2,1)} %copy-done.3, bf16[1024,128]{1,0:T(8,128)(2,1)} %get-tuple-element.9.code_ref, bf16[512,512]{1,0:T(8,128)(2,1)} %key_up_hbm.1, bf16[512,512]{1,0:T(8,128)(2,1)} %value_up_hbm.1), custom_call_target="tpu_custom_call" | custom-call | flops 1610612736 | bytes 4718592 | tf_op jit(solution)/shard_map/lift/pallas_call | solution.py:115
  46.0 5.3 %all-to-all-done = bf16[64,16,768]{2,0,1:T(8,128)(2,1)S(1)} async-done(((bf16[64,16,768]{2,0,1:T(8,128)(2,1)}), bf16[64,16,768]{2,0,1:T(8,128)(2,1)S(1)}, u32[]{:S(2)}, u32[]{:S(2)}) %all-to-all-start) | async-done | bytes 1572896 | tf_op jit(solution)/shard_map/all_to_all | solution.py:315
  51.2 0.0 copy-start.2
  51.2 0.0 collective-permute-done.prev_hbm
  51.3 1.1 %copy-done.2 = bf16[64,16,768]{2,0,1:T(8,128)(2,1)} copy-done((bf16[64,16,768]{2,0,1:T(8,128)(2,1)}, bf16[64,16,768]{2,0,1:T(8,128)(2,1)S(1)}, u32[]{:S(2)}) %copy-start.2) | copy-done | bytes 1572888
  52.4 11.8 %attend.1 = bf16[1024,512]{1,0:T(8,128)(2,1)} custom-call(s32[4]{0:T(128)} %and_select_fusion.1.first_ref, bf16[1024,768]{1,0:T(8,128)(2,1)} %bitcast.14, bf16[1024,128]{1,0:T(8,128)(2,1)} %select_convert_fusion.1.code_hbm, bf16[16,288,128]{2,1,0:T(8,128)(2,1)} %collective-permute-done.prev_hbm, bf16[1024,128]{1,0:T(8,128)(2,1)} %get-tuple-element.10.prev_code_hbm, ...), custom_call_target="tpu_custom_call" | custom-call | flops 8589934592 | bytes 8388608 | tf_op jit(solution)/shard_map/attend/pallas_call | solution.py:271
  64.2 22.1 %all_to_all.29 = bf16[16,64,512]{2,1,0:T(8,128)(2,1)S(1)} all-to-all(bf16[16,64,512]{2,1,0:T(8,128)(2,1)} %bitcast.15), channel_id=1, replica_groups=mesh['ctx'=32,'uly'=16] {'uly'}, dimensions={0} | all-to-all | bytes 2097152 | tf_op jit(solution)/shard_map/all_to_all | solution.py:322
  86.3 1.1 %copy.16 = bf16[16,8,8,512]{3,2,0,1:T(8,128)(2,1)} copy(bf16[16,8,8,512]{3,2,1,0:T(8,128)(2,1)S(1)} %bitcast.12) | data formatting | bytes 2097152 | tf_op jit(solution)/shard_map/reshape | solution.py:323
  (7 shorter events, 0.0 us)
Async XLA Ops:
  0.0 0.9 %copy-start = (bf16[64,576]{1,0:T(8,128)(2,1)S(1)}, bf16[64,576]{1,0:T(8,128)(2,1)}, u32[]{:S(2)}) copy-start(bf16[64,576]{1,0:T(8,128)(2,1)} %latent_ref.1) | copy-start | bytes 221188
  0.9 8.9 %copy-start.4 = (s32[128]{0:T(128)S(1)}, s32[128]{0:T(128)}, u32[]{:S(2)}) copy-start(s32[128]{0:T(128)} %param.9) | copy-start | bytes 1540
  2.0 8.2 %copy-start.1 = (bf16[64,12288]{1,0:T(8,128)(2,1)S(1)}, bf16[64,12288]{1,0:T(8,128)(2,1)}, u32[]{:S(2)}) copy-start(bf16[64,12288]{1,0:T(8,128)(2,1)} %param.5) | copy-start | bytes 4718596
  2.1 23.5 %all-to-all-start.1 = ((bf16[16,288,128]{2,1,0:T(8,128)(2,1)}), bf16[16,288,128]{2,1,0:T(8,128)(2,1)S(1)}, u32[]{:S(2)}, u32[]{:S(2)}) async-start(bf16[16,288,128]{2,1,0:T(8,128)(2,1)} %spread.1), calls=%async_computation.1 | async-start | bytes 2359296 | tf_op jit(solution)/shard_map/all_to_all | solution.py:313
  25.5 6.0 %copy-start.3 = (bf16[16,288,128]{2,1,0:T(8,128)(2,1)}, bf16[16,288,128]{2,1,0:T(8,128)(2,1)S(1)}, u32[]{:S(2)}) copy-start(bf16[16,288,128]{2,1,0:T(8,128)(2,1)S(1)} %all-to-all-done.1.packed_ref) | copy-start | bytes 3538948
  25.5 25.7 %all-to-all-start = ((bf16[64,16,768]{2,0,1:T(8,128)(2,1)}), bf16[64,16,768]{2,0,1:T(8,128)(2,1)S(1)}, u32[]{:S(2)}, u32[]{:S(2)}) async-start(bf16[64,16,768]{2,0,1:T(8,128)(2,1)} %bitcast.11), calls=%async_computation | async-start | bytes 3145728 | tf_op jit(solution)/shard_map/all_to_all | solution.py:315
  31.5 19.8 %collective-permute-start = (bf16[16,288,128]{2,1,0:T(8,128)(2,1)S(1)}, bf16[16,288,128]{2,1,0:T(8,128)(2,1)}, u32[]{:S(2)}, u32[]{:S(2)}) collective-permute-start(bf16[16,288,128]{2,1,0:T(8,128)(2,1)S(1)} %all-to-all-done.1.packed_ref), channel_id=1, source_target_pairs={{0,16},{16,32},{32,48},{48,64},{64,80},{80,96},{96,112},{112,128},... | collective-permute-start | bytes 3538952 | tf_op jit(solution)/shard_map/ppermute | solution.py:27
  51.2 1.1 %copy-start.2 = (bf16[64,16,768]{2,0,1:T(8,128)(2,1)}, bf16[64,16,768]{2,0,1:T(8,128)(2,1)S(1)}, u32[]{:S(2)}) copy-start(bf16[64,16,768]{2,0,1:T(8,128)(2,1)S(1)} %all-to-all-done) | copy-start | bytes 4718596

commit v4 on v3

--- a/solution.py
+++ b/solution.py
@@ -98,11 +98,11 @@
     return columns, values
 
 
-def lift_kernel(packed_ref, code_ref, key_up_ref, value_up_ref, key_ref, value_ref):
+def lift_kernel(packed_ref, code_ref, key_up_ref, value_up_ref, rows_ref):
     columns, values = lift_tile(packed_ref[...], code_ref[...], key_up_ref[...], value_up_ref[...])
     for i, column in enumerate(columns):
-        key_ref[:, i * 128 : (i + 1) * 128] = column
-    value_ref[...] = values
+        rows_ref[:, i * 128 : (i + 1) * 128] = column
+    rows_ref[:, len(columns) * 128 :] = values
 
 
 def lift(packed, code, key_up, value_up):
@@ -116,11 +116,8 @@
         lift_kernel,
         grid=(steps,),
         in_specs=[packed_spec, tiled(2 * CODE), whole(key_up), whole(value_up)],
-        out_specs=[tiled(key_cols), tiled(value_cols)],
-        out_shape=[
-            jax.ShapeDtypeStruct((rows, key_cols), jnp.bfloat16),
-            jax.ShapeDtypeStruct((rows, value_cols), jnp.bfloat16),
-        ],
+        out_specs=tiled(key_cols + value_cols),
+        out_shape=jax.ShapeDtypeStruct((rows, key_cols + value_cols), jnp.bfloat16),
         compiler_params=pltpu.CompilerParams(vmem_limit_bytes=60 * MIB),
         cost_estimate=pl.CostEstimate(
             flops=2 * rows * LATENT * (key_cols + value_cols),
@@ -132,13 +129,14 @@
 
 
 def attend_kernel(
-    first_ref, query_hbm, code_hbm, prev_hbm, prev_code_hbm, key_up_hbm, value_up_hbm, key_own,
-    value_own, out_hbm, query_ref, code_ref, prev_ref, prev_code_ref, key_up_ref, value_up_ref,
+    first_ref, query_hbm, code_hbm, prev_hbm, prev_code_hbm, key_up_hbm, value_up_hbm, own_hbm,
+    out_hbm, query_ref, code_ref, prev_ref, prev_code_ref, key_up_ref, value_up_ref,
     key_ref, value_ref, out_ref, key_sems, value_sems, query_sems, out_sems, lift_sems, prev_sems,
     code_sem,
 ):
     tiles = query_ref.shape[0] // TILE
     heads = value_ref.shape[1] // VDIM
+    key_cols = key_ref.shape[1]
     to_log2 = math.log2(math.e) / math.sqrt(HEAD)
     first_tile = first_ref[0]
 
@@ -148,8 +146,12 @@
     def key_copies(tile):
         here, there = tile_rows(tile), tile_rows(tiles + tile)
         return (
-            pltpu.make_async_copy(key_own.at[here], key_ref.at[there], key_sems.at[tile]),
-            pltpu.make_async_copy(value_own.at[here], value_ref.at[there], value_sems.at[tile]),
+            pltpu.make_async_copy(
+                own_hbm.at[here, :key_cols], key_ref.at[there], key_sems.at[tile]
+            ),
+            pltpu.make_async_copy(
+                own_hbm.at[here, key_cols:], value_ref.at[there], value_sems.at[tile]
+            ),
         )
 
     def query_copy(tile):
@@ -262,15 +264,15 @@
         out_copy(tile).wait()
 
 
-def attend(first, query, code, prev, prev_code, key_up, value_up, key_own, value_own):
-    rows, key_cols = key_own.shape
-    value_cols = value_own.shape[1]
+def attend(first, query, code, prev, prev_code, key_up, value_up, own):
+    rows, value_cols = own.shape[0], value_up.shape[1]
+    key_cols = own.shape[1] - value_cols
     tiles = rows // TILE
     there = pl.BlockSpec(memory_space=pl.ANY)
     scratch = lambda *shape: pltpu.VMEM(shape, jnp.bfloat16)
     return pl.pallas_call(
         attend_kernel,
-        in_specs=[pl.BlockSpec(memory_space=pltpu.SMEM)] + [there] * 8,
+        in_specs=[pl.BlockSpec(memory_space=pltpu.SMEM)] + [there] * 7,
         out_specs=there,
         out_shape=jax.ShapeDtypeStruct((rows, value_cols), jnp.bfloat16),
         scratch_shapes=[
@@ -291,14 +293,14 @@
             pltpu.SemaphoreType.DMA((tiles,)),
             pltpu.SemaphoreType.DMA,
         ],
-        compiler_params=pltpu.CompilerParams(vmem_limit_bytes=60 * MIB),
+        compiler_params=pltpu.CompilerParams(vmem_limit_bytes=50 * MIB),
         cost_estimate=pl.CostEstimate(
             flops=8 * rows * rows * key_cols,
             bytes_accessed=2 * rows * (2 * key_cols + 4 * value_cols),
             transcendentals=rows * rows * 4,
         ),
         name="attend",
-    )(first, query, code, prev, prev_code, key_up, value_up, key_own, value_own)
+    )(first, query, code, prev, prev_code, key_up, value_up, own)
 
 
 def per_device(queries, latent, key_up, value_up, doc_lengths):
@@ -313,10 +315,10 @@
     own = lax.all_to_all(spread(latent, uly_count), "uly", split_axis=0, concat_axis=0)
     previous = passed_along(own, "ctx", 1)
     local_query = lax.all_to_all(queries, "uly", split_axis=1, concat_axis=0, tiled=True)
-    key_own, value_own = lift(own, key_code[block_rows:], key_up, value_up)
+    own_rows_lifted = lift(own, key_code[block_rows:], key_up, value_up)
     result = attend(
         first, local_query, query_code[block_rows:], previous, key_code[:block_rows], key_up, value_up,
-        key_own, value_own,
+        own_rows_lifted,
     )
     result = result.reshape(uly_count, own_rows, heads_dev * VDIM)
     result = lax.all_to_all(result, "uly", split_axis=0, concat_axis=0)

time: 87.9 us -> 84.5 us (0.961)
  Pallas kernels: 17.8 us -> 14.1 us
  blocking collectives: 22.1 us -> 23.4 us
  other arithmetic: 5.41 us -> 4.15 us
  local copies, waits for them, and re-layouts: 5.37 us -> 4.16 us
  starting transfers between devices: 19.4 us -> 20.6 us
    pallas_call x1, Pallas kernels: 11.8 us -> 7.87 us  [attend(): pl.pallas_call(attend_kernel, in_specs=[pl.BlockSpec(memory_space=pltpu.S...]
    ppermute x1, waiting for transfers between devices: 0.01 us -> 1.85 us  [passed_along(): return lax.ppermute(block, axis, route)]
    all_to_all x1, waiting for transfers between devices: 5.3 us -> 3.96 us  [per_device(): lax.all_to_all(queries, 'uly', split_axis=1, concat_axis=0, tiled=True)]
    all_to_all x1, blocking collectives: 22.1 us -> 23.4 us  [per_device(): result = lax.all_to_all(result, 'uly', split_axis=0, concat_axis=0)]
    ppermute x1, starting transfers between devices: 6.28 us -> 7.46 us  [passed_along(): return lax.ppermute(block, axis, route)]
    unnamed x10, local copies, waits for them, and re-layouts: 2.03 us -> 0.9 us
  transfers between devices with their start and end apart: 3 -> 3, of which waited for: 2 -> 3; matrix products, arithmetic and copies ran while one was open for 9% -> 8% of each run, Pallas kernels for 6% -> 6%
where the time goes in v4:
time: 84.5 us; the launch traced here: 83.9 us
  blocking collectives  23.4 us (28%)
  starting transfers between devices  20.6 us (24%)
  waiting for transfers between devices  17.3 us (20%)
  Pallas kernels  14.1 us (17%)
  local copies, waits for them, and re-layouts  4.16 us (5%)
  other arithmetic  4.15 us (5%)
    all_to_all x1, blocking collectives, per_device(): result = lax.all_to_all(result, 'uly', split_axis=0, concat_axis=0)  23.4 us
    all_to_all x1, waiting for transfers between devices, per_device(): lax.all_to_all(spread(latent, uly_count), 'uly', split_axis=0, concat_axi...  11.4 us
    pallas_call x1, Pallas kernels, attend(): pl.pallas_call(attend_kernel, in_specs=[pl.BlockSpec(memory_space=pltpu.S...  7.87 us
    all_to_all x1, starting transfers between devices, per_device(): lax.all_to_all(spread(latent, uly_count), 'uly', split_axis=0, concat_axi...  7.76 us
    ppermute x1, starting transfers between devices, passed_along(): return lax.ppermute(block, axis, route)  7.46 us
    all_to_all x1, starting transfers between devices, per_device(): lax.all_to_all(queries, 'uly', split_axis=1, concat_axis=0, tiled=True)  5.41 us
    pallas_call x1, Pallas kernels, lift(): pl.pallas_call(lift_kernel, grid=(steps,), in_specs=[packed_spec, tiled(2...  5.06 us
    all_to_all x1, waiting for transfers between devices, per_device(): lax.all_to_all(queries, 'uly', split_axis=1, concat_axis=0, tiled=True)  3.96 us
  transfers between devices with their start and end apart: 3, of which 3 were waited for; matrix products, arithmetic and copies ran while one was open for 8% of the time, Pallas kernels for 6%

profile of v4, /device:TPU:1, one launch (start us, length us, event | category | flops | bytes accessed | tf_op | source)
XLA Modules:
  0.0 83.9 jit_solution(710206973727197165)
XLA Ops:
  0.0 0.0 copy-start
  0.0 0.9 %copy-done = bf16[64,576]{1,0:T(8,128)(2,1)S(1)} copy-done((bf16[64,576]{1,0:T(8,128)(2,1)S(1)}, bf16[64,576]{1,0:T(8,128)(2,1)}, u32[]{:S(2)}) %copy-start) | copy-done | bytes 73752
  0.9 0.0 copy-start.4
  0.9 1.2 %spread.1 = bf16[16,288,128]{2,1,0:T(8,128)(2,1)} custom-call(bf16[64,576]{1,0:T(8,128)(2,1)S(1)} %copy-done), custom_call_target="tpu_custom_call" | custom-call | tf_op jit(solution)/shard_map/spread/pallas_call | solution.py:65
  2.1 0.0 copy-start.3
  2.1 7.8 %all-to-all-start.1 = ((bf16[16,288,128]{2,1,0:T(8,128)(2,1)}), bf16[16,288,128]{2,1,0:T(8,128)(2,1)}, u32[]{:S(2)}, u32[]{:S(2)}) async-start(bf16[16,288,128]{2,1,0:T(8,128)(2,1)} %spread.1), calls=%async_computation.1 | async-start | bytes 2359296 | tf_op jit(solution)/shard_map/all_to_all | solution.py:315
  9.8 0.0 copy-done.4
  9.9 0.1 copy.12
  10.0 0.2 reduce-window.8
  10.1 0.1 reduce
  10.3 0.0 copy-done.3
  10.3 1.3 %copy.18 = bf16[8,16,8,768]{3,2,0,1:T(8,128)(2,1)} copy(bf16[8,16,8,768]{3,2,1,0:T(8,128)(2,1)S(1)} %bitcast.14) | data formatting | bytes 3145728 | tf_op jit(solution)/shard_map/all_to_all | solution.py:317
  11.6 0.2 select_reduce_fusion
  11.8 0.6 convert_reduce_fusion
  12.5 1.2 %compare_or_fusion = pred[2048,128]{1,0:T(8,128)(4,1)S(1)} fusion(s32[128]{0:T(128)S(1)} %and_select_fusion, s32[2048]{0:T(1024)S(1)} %get-tuple-element.8, s32[2048]{0:T(1024)S(1)} %get-tuple-element.7), kind=kLoop, calls=%fused_computation.3 | loop fusion | flops 786432 | bytes 279040 | tf_op jit(solution)/shard_map/or | solution.py:36
  13.7 11.4 %all-to-all-done.1.packed_ref = bf16[16,288,128]{2,1,0:T(8,128)(2,1)} async-done(((bf16[16,288,128]{2,1,0:T(8,128)(2,1)}), bf16[16,288,128]{2,1,0:T(8,128)(2,1)}, u32[]{:S(2)}, u32[]{:S(2)}) %all-to-all-start.1) | async-done | bytes 1179680 | tf_op jit(solution)/shard_map/all_to_all | solution.py:315
  25.1 5.4 %all-to-all-start = ((bf16[64,16,768]{2,0,1:T(8,128)(2,1)}), bf16[64,16,768]{2,0,1:T(8,128)(2,1)}, u32[]{:S(2)}, u32[]{:S(2)}) async-start(bf16[64,16,768]{2,0,1:T(8,128)(2,1)} %bitcast.11), calls=%async_computation | async-start | bytes 3145728 | tf_op jit(solution)/shard_map/all_to_all | solution.py:317
  30.6 7.5 %collective-permute-start = (bf16[16,288,128]{2,1,0:T(8,128)(2,1)}, bf16[16,288,128]{2,1,0:T(8,128)(2,1)S(1)}, u32[]{:S(2)}, u32[]{:S(2)}) collective-permute-start(bf16[16,288,128]{2,1,0:T(8,128)(2,1)} %all-to-all-done.1.packed_ref), channel_id=1, source_target_pairs={{0,16},{16,32},{32,48},{48,64},{64,80},{80,96},{96,112},{112,128},... | collective-permute-start | bytes 3538952 | tf_op jit(solution)/shard_map/ppermute | solution.py:27
  38.0 0.1 select_convert_fusion.1.code_hbm
  38.1 1.7 %select_convert_fusion = bf16[2048,128]{1,0:T(8,128)(2,1)S(1)} fusion(pred[2048]{0:T(1024)(128)(4,1)S(1)} %broadcast_compare_fusion, pred[128]{0:T(512)(128)(4,1)S(1)} %and_or_fusion, s32[2048]{0:T(1024)S(1)} %get-tuple-element.8, s32[2048]{0:T(1024)S(1)} %get-tuple-element.7, s32[128]{0:T(128)S(1)} %and_select_fusion), kind=kLoop, calls=%fused_computation.1 | loop fusion | flops 2097152 | bytes 543360 | tf_op jit(solution)/shard_map/convert_element_type | solution.py:40
  39.9 0.7 fusion.3
  40.6 0.0 copy-start.1
  40.6 0.0 copy-start.2
  40.6 5.1 %lift.1.own_hbm = bf16[1024,1536]{1,0:T(8,128)(2,1)} custom-call(bf16[16,288,128]{2,1,0:T(8,128)(2,1)} %all-to-all-done.1.packed_ref, bf16[1024,128]{1,0:T(8,128)(2,1)} %get-tuple-element.5.code_ref, bf16[512,512]{1,0:T(8,128)(2,1)} %key_up_hbm.1, bf16[512,512]{1,0:T(8,128)(2,1)} %value_up_hbm.1), custom_call_target="tpu_custom_call" | custom-call | flops 1610612736 | bytes 4718592 | tf_op jit(solution)/shard_map/lift/pallas_call | solution.py:115
  45.7 4.0 %all-to-all-done = bf16[64,16,768]{2,0,1:T(8,128)(2,1)} async-done(((bf16[64,16,768]{2,0,1:T(8,128)(2,1)}), bf16[64,16,768]{2,0,1:T(8,128)(2,1)}, u32[]{:S(2)}, u32[]{:S(2)}) %all-to-all-start) | async-done | bytes 1572896 | tf_op jit(solution)/shard_map/all_to_all | solution.py:317
  49.6 1.9 %collective-permute-done.prev_hbm = bf16[16,288,128]{2,1,0:T(8,128)(2,1)S(1)} collective-permute-done((bf16[16,288,128]{2,1,0:T(8,128)(2,1)}, bf16[16,288,128]{2,1,0:T(8,128)(2,1)S(1)}, u32[]{:S(2)}, u32[]{:S(2)}) %collective-permute-start) | collective-permute-done | bytes 1179680 | tf_op jit(solution)/shard_map/ppermute | solution.py:27
  51.5 0.0 copy-done.1
  51.5 0.0 copy-done.2
  51.5 7.9 %attend.1 = bf16[1024,512]{1,0:T(8,128)(2,1)S(1)} custom-call(s32[4]{0:T(128)S(1)} %and_select_fusion.1.first_ref, bf16[1024,768]{1,0:T(8,128)(2,1)} %bitcast.2.query_hbm, bf16[1024,128]{1,0:T(8,128)(2,1)S(1)} %select_convert_fusion.1.code_hbm, bf16[16,288,128]{2,1,0:T(8,128)(2,1)S(1)} %collective-permute-done.prev_hbm, ...), custom_call_target="tpu_custom_call" | custom-call | flops 8589934592 | bytes 8388608 | tf_op jit(solution)/shard_map/attend/pallas_call | solution.py:273
  59.4 23.4 %all_to_all.29 = bf16[16,64,512]{2,1,0:T(8,128)(2,1)S(1)} all-to-all(bf16[16,64,512]{2,1,0:T(8,128)(2,1)S(1)} %bitcast.12), channel_id=1, replica_groups=mesh['ctx'=32,'uly'=16] {'uly'}, dimensions={0} | all-to-all | bytes 2097152 | tf_op jit(solution)/shard_map/all_to_all | solution.py:324
  82.8 1.1 %copy.16 = bf16[16,8,8,512]{3,2,0,1:T(8,128)(2,1)} copy(bf16[16,8,8,512]{3,2,1,0:T(8,128)(2,1)S(1)} %bitcast.13) | data formatting | bytes 2097152 | tf_op jit(solution)/shard_map/reshape | solution.py:325
  (8 shorter events, 0.1 us)
Async XLA Ops:
  0.0 0.9 %copy-start = (bf16[64,576]{1,0:T(8,128)(2,1)S(1)}, bf16[64,576]{1,0:T(8,128)(2,1)}, u32[]{:S(2)}) copy-start(bf16[64,576]{1,0:T(8,128)(2,1)} %latent_ref.1) | copy-start | bytes 221188
  0.9 9.0 %copy-start.4 = (s32[128]{0:T(128)S(1)}, s32[128]{0:T(128)}, u32[]{:S(2)}) copy-start(s32[128]{0:T(128)} %param.9) | copy-start | bytes 1540
  2.1 8.2 %copy-start.3 = (bf16[64,12288]{1,0:T(8,128)(2,1)S(1)}, bf16[64,12288]{1,0:T(8,128)(2,1)}, u32[]{:S(2)}) copy-start(bf16[64,12288]{1,0:T(8,128)(2,1)} %param.5) | copy-start | bytes 4718596
  2.1 23.1 %all-to-all-start.1 = ((bf16[16,288,128]{2,1,0:T(8,128)(2,1)}), bf16[16,288,128]{2,1,0:T(8,128)(2,1)}, u32[]{:S(2)}, u32[]{:S(2)}) async-start(bf16[16,288,128]{2,1,0:T(8,128)(2,1)} %spread.1), calls=%async_computation.1 | async-start | bytes 2359296 | tf_op jit(solution)/shard_map/all_to_all | solution.py:315
  25.1 24.5 %all-to-all-start = ((bf16[64,16,768]{2,0,1:T(8,128)(2,1)}), bf16[64,16,768]{2,0,1:T(8,128)(2,1)}, u32[]{:S(2)}, u32[]{:S(2)}) async-start(bf16[64,16,768]{2,0,1:T(8,128)(2,1)} %bitcast.11), calls=%async_computation | async-start | bytes 3145728 | tf_op jit(solution)/shard_map/all_to_all | solution.py:317
  30.6 20.9 %collective-permute-start = (bf16[16,288,128]{2,1,0:T(8,128)(2,1)}, bf16[16,288,128]{2,1,0:T(8,128)(2,1)S(1)}, u32[]{:S(2)}, u32[]{:S(2)}) collective-permute-start(bf16[16,288,128]{2,1,0:T(8,128)(2,1)} %all-to-all-done.1.packed_ref), channel_id=1, source_target_pairs={{0,16},{16,32},{32,48},{48,64},{64,80},{80,96},{96,112},{112,128},... | collective-permute-start | bytes 3538952 | tf_op jit(solution)/shard_map/ppermute | solution.py:27
  40.6 10.9 %copy-start.1 = (bf16[512,512]{1,0:T(8,128)(2,1)S(1)}, bf16[512,512]{1,0:T(8,128)(2,1)}, u32[]{:S(2)}) copy-start(bf16[512,512]{1,0:T(8,128)(2,1)} %key_up_hbm.1) | copy-start | bytes 1572868
  40.6 10.9 %copy-start.2 = (bf16[512,512]{1,0:T(8,128)(2,1)S(1)}, bf16[512,512]{1,0:T(8,128)(2,1)}, u32[]{:S(2)}) copy-start(bf16[512,512]{1,0:T(8,128)(2,1)} %value_up_hbm.1) | copy-start | bytes 1572868

commit v5 on v4

--- a/solution.py
+++ b/solution.py
@@ -21,10 +21,9 @@
 MIB = 1 << 20
 
 
-def passed_along(block, axis, distance):
-    devices = range(lax.axis_size(axis))
-    route = [(i - distance, i) for i in devices if i - distance in devices]
-    return lax.ppermute(block, axis, route)
+def passed_along(block, axis, senders):
+    last = lax.axis_size(axis) - 1
+    return lax.ppermute(block, axis, [(i, i + 1) for i in senders if i < last])
 
 
 def doc_codes(doc_lengths, first, rows):
@@ -129,7 +128,7 @@
 
 
 def attend_kernel(
-    first_ref, query_hbm, code_hbm, prev_hbm, prev_code_hbm, key_up_hbm, value_up_hbm, own_hbm,
+    first_ref, query_hbm, code_hbm, far_hbm, near_hbm, prev_code_hbm, key_up_hbm, value_up_hbm, own_hbm,
     out_hbm, query_ref, code_ref, prev_ref, prev_code_ref, key_up_ref, value_up_ref,
     key_ref, value_ref, out_ref, key_sems, value_sems, query_sems, out_sems, lift_sems, prev_sems,
     code_sem,
@@ -164,9 +163,11 @@
 
     share = prev_ref.shape[0] // tiles
 
-    def prev_copy(tile):
+    odd = first_ref[tiles] == 1
+
+    def prev_copy(source, tile):
         here = pl.ds(tile * share, share)
-        return pltpu.make_async_copy(prev_hbm.at[here], prev_ref.at[here], prev_sems.at[tile])
+        return pltpu.make_async_copy(source.at[here], prev_ref.at[here], prev_sems.at[tile])
 
     lift_copies = [
         pltpu.make_async_copy(source, target, lift_sems.at[i])
@@ -181,7 +182,9 @@
         for copy in lift_copies:
             copy.start()
         for tile in range(tiles):
-            pl.when(first_tile <= tile)(lambda tile=tile: prev_copy(tile).start())
+            needed = first_tile <= tile
+            pl.when(needed & odd)(lambda tile=tile: prev_copy(near_hbm, tile).start())
+            pl.when(needed & ~odd)(lambda tile=tile: prev_copy(far_hbm, tile).start())
 
     code_copy.start()
     for tile in range(tiles):
@@ -196,7 +199,7 @@
 
     @pl.loop(jnp.minimum(first_tile, tiles), tiles)
     def _(tile):
-        prev_copy(tile).wait()
+        prev_copy(near_hbm, tile).wait()
         rows = tile_rows(tile)
         packed = prev_ref[pl.ds(tile * share, share)]
         columns, values = lift_tile(packed, prev_code_ref[rows, :], key_up_ref[...], value_up_ref[...])
@@ -264,7 +267,7 @@
         out_copy(tile).wait()
 
 
-def attend(first, query, code, prev, prev_code, key_up, value_up, own):
+def attend(first, query, code, near, far, prev_code, key_up, value_up, own):
     rows, value_cols = own.shape[0], value_up.shape[1]
     key_cols = own.shape[1] - value_cols
     tiles = rows // TILE
@@ -272,13 +275,13 @@
     scratch = lambda *shape: pltpu.VMEM(shape, jnp.bfloat16)
     return pl.pallas_call(
         attend_kernel,
-        in_specs=[pl.BlockSpec(memory_space=pltpu.SMEM)] + [there] * 7,
+        in_specs=[pl.BlockSpec(memory_space=pltpu.SMEM)] + [there] * 8,
         out_specs=there,
         out_shape=jax.ShapeDtypeStruct((rows, value_cols), jnp.bfloat16),
         scratch_shapes=[
             scratch(*query.shape),
             scratch(*code.shape),
-            scratch(*prev.shape),
+            scratch(*near.shape),
             scratch(*prev_code.shape),
             scratch(*key_up.shape),
             scratch(*value_up.shape),
@@ -300,7 +303,7 @@
             transcendentals=rows * rows * 4,
         ),
         name="attend",
-    )(first, query, code, prev, prev_code, key_up, value_up, own)
+    )(first, query, code, far, near, prev_code, key_up, value_up, own)
 
 
 def per_device(queries, latent, key_up, value_up, doc_lengths):
@@ -309,15 +312,33 @@
     block_rows = own_rows * uly_count
     heads_dev = key_up.shape[1] // NOPE
     block_start = lax.axis_index("ctx") * block_rows
-    query_code, key_code = doc_codes(doc_lengths, block_start - block_rows, 2 * block_rows)
-    first = first_tiles(doc_lengths, block_start, block_rows)
+    ctx = lax.axis_index("ctx")
+    parity = (ctx % 2).astype(jnp.int32)
+
+    def prepare(lengths, rows):
+        parts = rows.reshape(own_rows, uly_count, -1).transpose(1, 0, 2)
+        codes = doc_codes(lengths, block_start - block_rows, 2 * block_rows)
+        first = first_tiles(lengths, block_start, block_rows)
+        return parts, codes[0][block_rows:], codes[1], jnp.concatenate([first, parity[None]])
+
+    late = (parity == 1) & (ctx > 1)
+    shapes = jax.eval_shape(prepare, doc_lengths, queries)
+    skip = lambda *_: tuple(jnp.zeros(a.shape, a.dtype) for a in shapes)
+    early = lax.cond(late, prepare, skip, doc_lengths, queries)
+    latent, early = lax.optimization_barrier((latent, early))
 
     own = lax.all_to_all(spread(latent, uly_count), "uly", split_axis=0, concat_axis=0)
-    previous = passed_along(own, "ctx", 1)
-    local_query = lax.all_to_all(queries, "uly", split_axis=1, concat_axis=0, tiled=True)
+    parts, query_code, key_code, first = lax.cond(
+        late, lambda held, *_: held, lambda _, *given: prepare(*given), early, doc_lengths, queries
+    )
+    ctx_count = lax.axis_size("ctx")
+    far = passed_along(own, "ctx", range(1, ctx_count, 2))
+    near = passed_along(own, "ctx", range(0, ctx_count, 2))
+    local_query = lax.all_to_all(parts, "uly", split_axis=0, concat_axis=0)
+    local_query = local_query.reshape(block_rows, -1)
     own_rows_lifted = lift(own, key_code[block_rows:], key_up, value_up)
     result = attend(
-        first, local_query, query_code[block_rows:], previous, key_code[:block_rows], key_up, value_up,
+        first, local_query, query_code, near, far, key_code[:block_rows], key_up, value_up,
         own_rows_lifted,
     )
     result = result.reshape(uly_count, own_rows, heads_dev * VDIM)

time: 84.5 us -> 84.7 us (level)
  starting transfers between devices: 20.6 us -> 16.9 us
  Pallas kernels: 14.1 us -> 15.3 us
  local copies, waits for them, and re-layouts: 4.16 us -> 5.02 us
    all_to_all x1, waiting for transfers between devices: 3.96 us -> 10.1 us  [per_device(): local_query = lax.all_to_all(parts, 'uly', split_axis=0, concat_axis=0)]
    ppermute x1 -> x2, starting transfers between devices: 7.46 us -> 3.88 us  [passed_along(): return lax.ppermute(block, axis, [(i, i + 1) for i in senders if i < last])]
    all_to_all x1, waiting for transfers between devices: 11.4 us -> 7.99 us  [per_device(): lax.all_to_all(spread(latent, uly_count), 'uly', split_axis=0, concat_axi...]
    cond x0 -> x2, local copies, waits for them, and re-layouts: none -> 1.94 us  [the longest x1 1.64 us: per_device(): lax.cond(late, lambda held, *_: held, lambda _, *given: prepare(*given),...]
    ppermute x1 -> x2, waiting for transfers between devices: 1.85 us -> 0.01 us  [passed_along(): return lax.ppermute(block, axis, [(i, i + 1) for i in senders if i < last])]
    all_to_all x1 -> x0, local copies, waits for them, and re-layouts: 1.33 us -> none  [per_device(): lax.all_to_all(queries, 'uly', split_axis=1, concat_axis=0, tiled=True)]
    pallas_call x1, Pallas kernels: 7.87 us -> 9.05 us  [attend(): pl.pallas_call(attend_kernel, in_specs=[pl.BlockSpec(memory_space=pltpu.S...]
  transfers between devices with their start and end apart: 3 -> 4, of which waited for: 3 -> 2; matrix products, arithmetic and copies ran while one was open for 8% -> 9% of each run, Pallas kernels for 6% -> 6%
where the time goes in v5:
time: 84.7 us; the launch traced here: 83.3 us
  blocking collectives  23.5 us (28%)
  waiting for transfers between devices  18.1 us (21%)
  starting transfers between devices  16.9 us (20%)
  Pallas kernels  15.3 us (18%)
  local copies, waits for them, and re-layouts  5.02 us (6%)
  other arithmetic  4.22 us (5%)
    all_to_all x1, blocking collectives, per_device(): result = lax.all_to_all(result, 'uly', split_axis=0, concat_axis=0)  23.5 us
    all_to_all x1, waiting for transfers between devices, per_device(): local_query = lax.all_to_all(parts, 'uly', split_axis=0, concat_axis=0)  10.1 us
    pallas_call x1, Pallas kernels, attend(): pl.pallas_call(attend_kernel, in_specs=[pl.BlockSpec(memory_space=pltpu.S...  9.05 us
    all_to_all x1, waiting for transfers between devices, per_device(): lax.all_to_all(spread(latent, uly_count), 'uly', split_axis=0, concat_axi...  7.99 us
    all_to_all x1, starting transfers between devices, per_device(): lax.all_to_all(spread(latent, uly_count), 'uly', split_axis=0, concat_axi...  7.63 us
    all_to_all x1, starting transfers between devices, per_device(): local_query = lax.all_to_all(parts, 'uly', split_axis=0, concat_axis=0)  5.43 us
    pallas_call x1, Pallas kernels, lift(): pl.pallas_call(lift_kernel, grid=(steps,), in_specs=[packed_spec, tiled(2...  5.06 us
    ppermute x2, starting transfers between devices, passed_along(): return lax.ppermute(block, axis, [(i, i + 1) for i in senders if i < last])  3.88 us
  transfers between devices with their start and end apart: 4, of which 2 were waited for; matrix products, arithmetic and copies ran while one was open for 9% of the time, Pallas kernels for 6%

profile of v5, /device:TPU:1, one launch (start us, length us, event | category | flops | bytes accessed | tf_op | source)
XLA Modules:
  0.0 83.3 jit_solution(12621870244314923397)
XLA Ops:
  0.0 0.2 conditional.2
  0.0 0.1 broadcast.325
  0.1 0.1 broadcast.327
  0.3 0.0 copy-start.4
  0.3 0.8 copy-done.4
  1.1 1.2 %spread.1 = bf16[16,288,128]{2,1,0:T(8,128)(2,1)} custom-call(bf16[64,576]{1,0:T(8,128)(2,1)S(1)} %copy-done), custom_call_target="tpu_custom_call" | custom-call | tf_op jit(solution)/shard_map/spread/pallas_call | solution.py:64
  2.2 7.6 %all-to-all-start.1 = ((bf16[16,288,128]{2,1,0:T(8,128)(2,1)}), bf16[16,288,128]{2,1,0:T(8,128)(2,1)}, u32[]{:S(2)}, u32[]{:S(2)}) async-start(bf16[16,288,128]{2,1,0:T(8,128)(2,1)} %spread.1), calls=%async_computation.1 | async-start | bytes 2359296 | tf_op jit(solution)/shard_map/all_to_all | solution.py:330
  9.9 5.6 %conditional.3 = (bf16[16,64,768]{2,0,1:T(8,128)(2,1)S(1)}, bf16[1024,128]{1,0:T(8,128)(2,1)S(1)}, s32[5]{0:T(128)S(1)}, bf16[1024,128]{1,0:T(8,128)(2,1)}, bf16[1024,128]{1,0:T(8,128)(2,1)}) conditional(s32[]{:T(128)} %convert_element_type.25, (bf16[64,12288]{1,0:T(8,128)(2,1)S(1)}, s32[128]{0:T(128)S(1)}, s32[]{:T(128)}, s32[]{:T(128)}) %tuple.42, ...), branch_computations={%region_5.9_spmd, %region_9.10_spmd} | conditional | flops 3997386 | bytes 5467588 | solution.py:331
  9.9 0.1 copy.19
  10.0 0.2 reduce-window.16
  10.2 0.1 reduce.1
  10.3 0.6 convert_reduce_fusion.1
  11.0 1.7 %select_convert_fusion.2 = bf16[2048,128]{1,0:T(8,128)(2,1)S(1)} fusion(pred[2048]{0:T(1024)(128)(4,1)S(1)} %broadcast_compare_fusion.1, pred[128]{0:T(512)(128)(4,1)S(1)} %and_or_fusion.1, s32[2048]{0:T(1024)S(1)} %get-tuple-element.100, s32[2048]{0:T(1024)S(1)} %get-tuple-element.99, s32[128]{0:T(128)S(1)} %and_select_fusion.3), kind=kLoop, calls=%fused_computation.24 | loop fusion | flops 2097152 | bytes 543360 | tf_op jit(solution)/shard_map/cond/branch_0_fun/convert_element_type | solution.py:39
  12.7 0.9 %fusion.7 = (bf16[1024,128]{1,0:T(8,128)(2,1)}, bf16[1024,128]{1,0:T(8,128)(2,1)}) fusion(bf16[2048,128]{1,0:T(8,128)(2,1)S(1)} %select_convert_fusion.2), kind=kLoop, calls=%fused_computation.49 | loop fusion | bytes 1048576 | tf_op jit(solution)/shard_map/slice | solution.py:339
  13.6 1.2 %compare_or_fusion.1 = pred[2048,128]{1,0:T(8,128)(4,1)S(1)} fusion(s32[128]{0:T(128)S(1)} %and_select_fusion.3, s32[2048]{0:T(1024)S(1)} %get-tuple-element.100, s32[2048]{0:T(1024)S(1)} %get-tuple-element.99), kind=kLoop, calls=%fused_computation.26 | loop fusion | flops 786432 | bytes 279040 | tf_op jit(solution)/shard_map/cond/branch_0_fun/or | solution.py:35
  14.8 0.1 select_convert_fusion.3
  14.9 0.2 select_reduce_fusion.1
  15.1 0.1 pad_add_fusion.1
  15.2 0.3 copy.23
  15.5 1.6 %copy.20 = bf16[16,64,768]{2,1,0:T(8,128)(2,1)} copy(bf16[16,64,768]{2,0,1:T(8,128)(2,1)S(1)} %get-tuple-element.88) | data formatting | bytes 3145728 | tf_op jit(solution)/shard_map/cond | solution.py:331
  17.1 8.0 %all-to-all-done.1.packed_ref = bf16[16,288,128]{2,1,0:T(8,128)(2,1)} async-done(((bf16[16,288,128]{2,1,0:T(8,128)(2,1)}), bf16[16,288,128]{2,1,0:T(8,128)(2,1)}, u32[]{:S(2)}, u32[]{:S(2)}) %all-to-all-start.1) | async-done | bytes 1179680 | tf_op jit(solution)/shard_map/all_to_all | solution.py:330
  25.1 5.4 %all-to-all-start = ((bf16[16,64,768]{2,1,0:T(8,128)(2,1)}), bf16[16,64,768]{2,1,0:T(8,128)(2,1)}, u32[]{:S(2)}, u32[]{:S(2)}) async-start(bf16[16,64,768]{2,1,0:T(8,128)(2,1)} %copy.20), calls=%async_computation | async-start | bytes 3145728 | tf_op jit(solution)/shard_map/all_to_all | solution.py:337
  30.6 2.6 %collective-permute-start = (bf16[16,288,128]{2,1,0:T(8,128)(2,1)}, bf16[16,288,128]{2,1,0:T(8,128)(2,1)S(1)}, u32[]{:S(2)}, u32[]{:S(2)}) collective-permute-start(bf16[16,288,128]{2,1,0:T(8,128)(2,1)} %all-to-all-done.1.packed_ref), channel_id=1, source_target_pairs={{16,32},{48,64},{80,96},{112,128},{144,160},{176,192},{208,224},{2... | collective-permute-start | bytes 3538952 | tf_op jit(solution)/shard_map/ppermute | solution.py:26
  33.2 1.3 %collective-permute-start.1 = (bf16[16,288,128]{2,1,0:T(8,128)(2,1)}, bf16[16,288,128]{2,1,0:T(8,128)(2,1)}, u32[]{:S(2)}, u32[]{:S(2)}) collective-permute-start(bf16[16,288,128]{2,1,0:T(8,128)(2,1)} %all-to-all-done.1.packed_ref), channel_id=1, source_target_pairs={{0,16},{32,48},{64,80},{96,112},{128,144},{160,176},{192,208},{224... | collective-permute-start | bytes 3538952 | tf_op jit(solution)/shard_map/ppermute | solution.py:26
  34.5 0.0 copy-start.1
  34.5 0.0 copy-start.2
  34.5 5.1 %lift.1.own_hbm = bf16[1024,1536]{1,0:T(8,128)(2,1)} custom-call(bf16[16,288,128]{2,1,0:T(8,128)(2,1)} %all-to-all-done.1.packed_ref, bf16[1024,128]{1,0:T(8,128)(2,1)} %get-tuple-element.92.code_ref, bf16[512,512]{1,0:T(8,128)(2,1)} %key_up_hbm.1, bf16[512,512]{1,0:T(8,128)(2,1)} %value_up_hbm.1), custom_call_target="tpu_custom_call" | custom-call | flops 1610612736 | bytes 4718592 | tf_op jit(solution)/shard_map/lift/pallas_call | solution.py:114
  39.5 10.1 %all-to-all-done = bf16[16,64,768]{2,1,0:T(8,128)(2,1)} async-done(((bf16[16,64,768]{2,1,0:T(8,128)(2,1)}), bf16[16,64,768]{2,1,0:T(8,128)(2,1)}, u32[]{:S(2)}, u32[]{:S(2)}) %all-to-all-start) | async-done | bytes 1572896 | tf_op jit(solution)/shard_map/all_to_all | solution.py:337
  49.6 0.0 collective-permute-done.far_hbm
  49.6 9.0 %attend.1 = bf16[1024,512]{1,0:T(8,128)(2,1)S(1)} custom-call(s32[5]{0:T(128)S(1)} %get-tuple-element.87.first_ref, bf16[1024,768]{1,0:T(8,128)(2,1)} %bitcast.6.query_hbm, bf16[1024,128]{1,0:T(8,128)(2,1)S(1)} %get-tuple-element.89.code_hbm, bf16[16,288,128]{2,1,0:T(8,128)(2,1)S(1)} %collective-permute-done.far_hbm, ...), custom_call_target="tpu_custom_call" | custom-call | flops 8589934592 | bytes 8388608 | tf_op jit(solution)/shard_map/attend/pallas_call | solution.py:276
  58.7 23.5 %all_to_all.15 = bf16[16,64,512]{2,1,0:T(8,128)(2,1)S(1)} all-to-all(bf16[16,64,512]{2,1,0:T(8,128)(2,1)S(1)} %bitcast.17), channel_id=1, replica_groups=mesh['ctx'=32,'uly'=16] {'uly'}, dimensions={0} | all-to-all | bytes 2097152 | tf_op jit(solution)/shard_map/all_to_all | solution.py:345
  82.2 1.1 %copy.24 = bf16[16,8,8,512]{3,2,0,1:T(8,128)(2,1)} copy(bf16[16,8,8,512]{3,2,1,0:T(8,128)(2,1)S(1)} %bitcast.22) | data formatting | bytes 2097152 | tf_op jit(solution)/shard_map/reshape | solution.py:346
  (19 shorter events, 0.1 us)
Async XLA Ops:
  0.0 1.0 %copy-start = (bf16[64,576]{1,0:T(8,128)(2,1)S(1)}, bf16[64,576]{1,0:T(8,128)(2,1)}, u32[]{:S(2)}) copy-start(bf16[64,576]{1,0:T(8,128)(2,1)} %latent_ref) | copy-start | bytes 221188
  0.3 0.8 copy-start.4
  1.1 8.8 %copy-start.3 = (bf16[64,12288]{1,0:T(8,128)(2,1)S(1)}, bf16[64,12288]{1,0:T(8,128)(2,1)}, u32[]{:S(2)}) copy-start(bf16[64,12288]{1,0:T(8,128)(2,1)} %param.9) | copy-start | bytes 4718596
  1.1 8.8 %copy-start.5 = (s32[128]{0:T(128)S(1)}, s32[128]{0:T(128)}, u32[]{:S(2)}) copy-start(s32[128]{0:T(128)} %param.13) | copy-start | bytes 1540
  2.2 22.9 %all-to-all-start.1 = ((bf16[16,288,128]{2,1,0:T(8,128)(2,1)}), bf16[16,288,128]{2,1,0:T(8,128)(2,1)}, u32[]{:S(2)}, u32[]{:S(2)}) async-start(bf16[16,288,128]{2,1,0:T(8,128)(2,1)} %spread.1), calls=%async_computation.1 | async-start | bytes 2359296 | tf_op jit(solution)/shard_map/all_to_all | solution.py:330
  25.1 24.5 %all-to-all-start = ((bf16[16,64,768]{2,1,0:T(8,128)(2,1)}), bf16[16,64,768]{2,1,0:T(8,128)(2,1)}, u32[]{:S(2)}, u32[]{:S(2)}) async-start(bf16[16,64,768]{2,1,0:T(8,128)(2,1)} %copy.20), calls=%async_computation | async-start | bytes 3145728 | tf_op jit(solution)/shard_map/all_to_all | solution.py:337
  30.6 19.1 %collective-permute-start = (bf16[16,288,128]{2,1,0:T(8,128)(2,1)}, bf16[16,288,128]{2,1,0:T(8,128)(2,1)S(1)}, u32[]{:S(2)}, u32[]{:S(2)}) collective-permute-start(bf16[16,288,128]{2,1,0:T(8,128)(2,1)} %all-to-all-done.1.packed_ref), channel_id=1, source_target_pairs={{16,32},{48,64},{80,96},{112,128},{144,160},{176,192},{208,224},{2... | collective-permute-start | bytes 3538952 | tf_op jit(solution)/shard_map/ppermute | solution.py:26
  33.2 16.5 %collective-permute-start.1 = (bf16[16,288,128]{2,1,0:T(8,128)(2,1)}, bf16[16,288,128]{2,1,0:T(8,128)(2,1)}, u32[]{:S(2)}, u32[]{:S(2)}) collective-permute-start(bf16[16,288,128]{2,1,0:T(8,128)(2,1)} %all-to-all-done.1.packed_ref), channel_id=1, source_target_pairs={{0,16},{32,48},{64,80},{96,112},{128,144},{160,176},{192,208},{224... | collective-permute-start | bytes 3538952 | tf_op jit(solution)/shard_map/ppermute | solution.py:26
  34.5 15.2 %copy-start.1 = (bf16[512,512]{1,0:T(8,128)(2,1)S(1)}, bf16[512,512]{1,0:T(8,128)(2,1)}, u32[]{:S(2)}) copy-start(bf16[512,512]{1,0:T(8,128)(2,1)} %key_up_hbm.1) | copy-start | bytes 1572868
  34.5 15.2 %copy-start.2 = (bf16[512,512]{1,0:T(8,128)(2,1)S(1)}, bf16[512,512]{1,0:T(8,128)(2,1)}, u32[]{:S(2)}) copy-start(bf16[512,512]{1,0:T(8,128)(2,1)} %value_up_hbm.1) | copy-start | bytes 1572868

commit v6 on v5

--- a/solution.py
+++ b/solution.py
@@ -129,8 +129,8 @@
 
 def attend_kernel(
     first_ref, query_hbm, code_hbm, far_hbm, near_hbm, prev_code_hbm, key_up_hbm, value_up_hbm, own_hbm,
-    out_hbm, query_ref, code_ref, prev_ref, prev_code_ref, key_up_ref, value_up_ref,
-    key_ref, value_ref, out_ref, key_sems, value_sems, query_sems, out_sems, lift_sems, prev_sems,
+    out_ref, query_ref, code_ref, prev_ref, prev_code_ref, key_up_ref, value_up_ref,
+    key_ref, value_ref, key_sems, value_sems, query_sems, lift_sems, prev_sems,
     code_sem,
 ):
     tiles = query_ref.shape[0] // TILE
@@ -156,10 +156,6 @@
     def query_copy(tile):
         here = tile_rows(tile)
         return pltpu.make_async_copy(query_hbm.at[here], query_ref.at[here], query_sems.at[tile])
-
-    def out_copy(tile):
-        here = tile_rows(tile)
-        return pltpu.make_async_copy(out_ref.at[here], out_hbm.at[here], out_sems.at[tile])
 
     share = prev_ref.shape[0] // tiles
 
@@ -261,10 +257,6 @@
         count = tiles + 1 + step - first_ref[step]
         for n in range(1, tiles + 2):
             pl.when(count == n)(functools.partial(attend_rows, step, n))
-        out_copy(step).start()
-
-    for tile in range(tiles):
-        out_copy(tile).wait()
 
 
 def attend(first, query, code, near, far, prev_code, key_up, value_up, own):
@@ -276,7 +268,7 @@
     return pl.pallas_call(
         attend_kernel,
         in_specs=[pl.BlockSpec(memory_space=pltpu.SMEM)] + [there] * 8,
-        out_specs=there,
+        out_specs=pl.BlockSpec(memory_space=pltpu.VMEM),
         out_shape=jax.ShapeDtypeStruct((rows, value_cols), jnp.bfloat16),
         scratch_shapes=[
             scratch(*query.shape),
@@ -287,8 +279,6 @@
             scratch(*value_up.shape),
             scratch(2 * rows, key_cols),
             scratch(2 * rows, value_cols),
-            scratch(rows, value_cols),
-            pltpu.SemaphoreType.DMA((tiles,)),
             pltpu.SemaphoreType.DMA((tiles,)),
             pltpu.SemaphoreType.DMA((tiles,)),
             pltpu.SemaphoreType.DMA((tiles,)),

time: 84.7 us -> 84 us (level); the launches traced: 83.3 us -> 83.8 us
  no operation moved by 1% of the time
where the time goes in v6:
time: 84 us; the launch traced here: 83.8 us
  blocking collectives  23.4 us (28%)
  waiting for transfers between devices  18.1 us (22%)
  starting transfers between devices  16.9 us (20%)
  Pallas kernels  15.9 us (19%)
  local copies, waits for them, and re-layouts  5.02 us (6%)
  other arithmetic  4.22 us (5%)
    all_to_all x1, blocking collectives, per_device(): result = lax.all_to_all(result, 'uly', split_axis=0, concat_axis=0)  23.4 us
    all_to_all x1, waiting for transfers between devices, per_device(): local_query = lax.all_to_all(parts, 'uly', split_axis=0, concat_axis=0)  10.1 us
    pallas_call x1, Pallas kernels, attend(): pl.pallas_call(attend_kernel, in_specs=[pl.BlockSpec(memory_space=pltpu.S...  9.68 us
    all_to_all x1, waiting for transfers between devices, per_device(): lax.all_to_all(spread(latent, uly_count), 'uly', split_axis=0, concat_axi...  7.99 us
    all_to_all x1, starting transfers between devices, per_device(): lax.all_to_all(spread(latent, uly_count), 'uly', split_axis=0, concat_axi...  7.63 us
    all_to_all x1, starting transfers between devices, per_device(): local_query = lax.all_to_all(parts, 'uly', split_axis=0, concat_axis=0)  5.43 us
    pallas_call x1, Pallas kernels, lift(): pl.pallas_call(lift_kernel, grid=(steps,), in_specs=[packed_spec, tiled(2...  5.06 us
    ppermute x2, starting transfers between devices, passed_along(): return lax.ppermute(block, axis, [(i, i + 1) for i in senders if i < last])  3.88 us
  transfers between devices with their start and end apart: 4, of which 2 were waited for; matrix products, arithmetic and copies ran while one was open for 9% of the time, Pallas kernels for 6%

profile of v6, /device:TPU:1, one launch (start us, length us, event | category | flops | bytes accessed | tf_op | source)
XLA Modules:
  0.0 83.8 jit_solution(4229326928398295637)
XLA Ops:
  0.0 0.2 conditional.2
  0.0 0.1 broadcast.325
  0.1 0.1 broadcast.327
  0.3 0.0 copy-start.4
  0.3 0.8 copy-done.4
  1.1 1.2 %spread.1 = bf16[16,288,128]{2,1,0:T(8,128)(2,1)} custom-call(bf16[64,576]{1,0:T(8,128)(2,1)S(1)} %copy-done), custom_call_target="tpu_custom_call" | custom-call | tf_op jit(solution)/shard_map/spread/pallas_call | solution.py:64
  2.2 7.6 %all-to-all-start.1 = ((bf16[16,288,128]{2,1,0:T(8,128)(2,1)}), bf16[16,288,128]{2,1,0:T(8,128)(2,1)}, u32[]{:S(2)}, u32[]{:S(2)}) async-start(bf16[16,288,128]{2,1,0:T(8,128)(2,1)} %spread.1), calls=%async_computation.1 | async-start | bytes 2359296 | tf_op jit(solution)/shard_map/all_to_all | solution.py:320
  9.9 5.6 %conditional.3 = (bf16[16,64,768]{2,0,1:T(8,128)(2,1)S(1)}, bf16[1024,128]{1,0:T(8,128)(2,1)S(1)}, s32[5]{0:T(128)S(1)}, bf16[1024,128]{1,0:T(8,128)(2,1)}, bf16[1024,128]{1,0:T(8,128)(2,1)}) conditional(s32[]{:T(128)} %convert_element_type.25, (bf16[64,12288]{1,0:T(8,128)(2,1)S(1)}, s32[128]{0:T(128)S(1)}, s32[]{:T(128)}, s32[]{:T(128)}) %tuple.42, ...), branch_computations={%region_5.9_spmd, %region_9.10_spmd} | conditional | flops 3997386 | bytes 5467588 | solution.py:321
  9.9 0.1 copy.19
  10.0 0.2 reduce-window.16
  10.2 0.1 reduce.1
  10.3 0.6 convert_reduce_fusion.1
  11.0 1.7 %select_convert_fusion.2 = bf16[2048,128]{1,0:T(8,128)(2,1)S(1)} fusion(pred[2048]{0:T(1024)(128)(4,1)S(1)} %broadcast_compare_fusion.1, pred[128]{0:T(512)(128)(4,1)S(1)} %and_or_fusion.1, s32[2048]{0:T(1024)S(1)} %get-tuple-element.100, s32[2048]{0:T(1024)S(1)} %get-tuple-element.99, s32[128]{0:T(128)S(1)} %and_select_fusion.3), kind=kLoop, calls=%fused_computation.24 | loop fusion | flops 2097152 | bytes 543360 | tf_op jit(solution)/shard_map/cond/branch_0_fun/convert_element_type | solution.py:39
  12.7 0.9 %fusion.7 = (bf16[1024,128]{1,0:T(8,128)(2,1)}, bf16[1024,128]{1,0:T(8,128)(2,1)}) fusion(bf16[2048,128]{1,0:T(8,128)(2,1)S(1)} %select_convert_fusion.2), kind=kLoop, calls=%fused_computation.49 | loop fusion | bytes 1048576 | tf_op jit(solution)/shard_map/slice | solution.py:329
  13.6 1.2 %compare_or_fusion.1 = pred[2048,128]{1,0:T(8,128)(4,1)S(1)} fusion(s32[128]{0:T(128)S(1)} %and_select_fusion.3, s32[2048]{0:T(1024)S(1)} %get-tuple-element.100, s32[2048]{0:T(1024)S(1)} %get-tuple-element.99), kind=kLoop, calls=%fused_computation.26 | loop fusion | flops 786432 | bytes 279040 | tf_op jit(solution)/shard_map/cond/branch_0_fun/or | solution.py:35
  14.8 0.1 select_convert_fusion.3
  14.9 0.2 select_reduce_fusion.1
  15.1 0.1 pad_add_fusion.1
  15.2 0.3 copy.23
  15.5 1.6 %copy.20 = bf16[16,64,768]{2,1,0:T(8,128)(2,1)} copy(bf16[16,64,768]{2,0,1:T(8,128)(2,1)S(1)} %get-tuple-element.88) | data formatting | bytes 3145728 | tf_op jit(solution)/shard_map/cond | solution.py:321
  17.1 8.0 %all-to-all-done.1.packed_ref = bf16[16,288,128]{2,1,0:T(8,128)(2,1)} async-done(((bf16[16,288,128]{2,1,0:T(8,128)(2,1)}), bf16[16,288,128]{2,1,0:T(8,128)(2,1)}, u32[]{:S(2)}, u32[]{:S(2)}) %all-to-all-start.1) | async-done | bytes 1179680 | tf_op jit(solution)/shard_map/all_to_all | solution.py:320
  25.1 5.4 %all-to-all-start = ((bf16[16,64,768]{2,1,0:T(8,128)(2,1)}), bf16[16,64,768]{2,1,0:T(8,128)(2,1)}, u32[]{:S(2)}, u32[]{:S(2)}) async-start(bf16[16,64,768]{2,1,0:T(8,128)(2,1)} %copy.20), calls=%async_computation | async-start | bytes 3145728 | tf_op jit(solution)/shard_map/all_to_all | solution.py:327
  30.6 2.6 %collective-permute-start = (bf16[16,288,128]{2,1,0:T(8,128)(2,1)}, bf16[16,288,128]{2,1,0:T(8,128)(2,1)S(1)}, u32[]{:S(2)}, u32[]{:S(2)}) collective-permute-start(bf16[16,288,128]{2,1,0:T(8,128)(2,1)} %all-to-all-done.1.packed_ref), channel_id=1, source_target_pairs={{16,32},{48,64},{80,96},{112,128},{144,160},{176,192},{208,224},{2... | collective-permute-start | bytes 3538952 | tf_op jit(solution)/shard_map/ppermute | solution.py:26
  33.2 1.3 %collective-permute-start.1 = (bf16[16,288,128]{2,1,0:T(8,128)(2,1)}, bf16[16,288,128]{2,1,0:T(8,128)(2,1)}, u32[]{:S(2)}, u32[]{:S(2)}) collective-permute-start(bf16[16,288,128]{2,1,0:T(8,128)(2,1)} %all-to-all-done.1.packed_ref), channel_id=1, source_target_pairs={{0,16},{32,48},{64,80},{96,112},{128,144},{160,176},{192,208},{224... | collective-permute-start | bytes 3538952 | tf_op jit(solution)/shard_map/ppermute | solution.py:26
  34.5 0.0 copy-start.1
  34.5 0.0 copy-start.2
  34.5 5.1 %lift.1.own_hbm = bf16[1024,1536]{1,0:T(8,128)(2,1)} custom-call(bf16[16,288,128]{2,1,0:T(8,128)(2,1)} %all-to-all-done.1.packed_ref, bf16[1024,128]{1,0:T(8,128)(2,1)} %get-tuple-element.92.code_ref, bf16[512,512]{1,0:T(8,128)(2,1)} %key_up_hbm.1, bf16[512,512]{1,0:T(8,128)(2,1)} %value_up_hbm.1), custom_call_target="tpu_custom_call" | custom-call | flops 1610612736 | bytes 4718592 | tf_op jit(solution)/shard_map/lift/pallas_call | solution.py:114
  39.5 10.1 %all-to-all-done = bf16[16,64,768]{2,1,0:T(8,128)(2,1)} async-done(((bf16[16,64,768]{2,1,0:T(8,128)(2,1)}), bf16[16,64,768]{2,1,0:T(8,128)(2,1)}, u32[]{:S(2)}, u32[]{:S(2)}) %all-to-all-start) | async-done | bytes 1572896 | tf_op jit(solution)/shard_map/all_to_all | solution.py:327
  49.6 0.0 collective-permute-done.far_hbm
  49.6 9.7 %attend.1 = bf16[1024,512]{1,0:T(8,128)(2,1)S(1)} custom-call(s32[5]{0:T(128)S(1)} %get-tuple-element.87.first_ref, bf16[1024,768]{1,0:T(8,128)(2,1)} %bitcast.6.query_hbm, bf16[1024,128]{1,0:T(8,128)(2,1)S(1)} %get-tuple-element.89.code_hbm, bf16[16,288,128]{2,1,0:T(8,128)(2,1)S(1)} %collective-permute-done.far_hbm, ...), custom_call_target="tpu_custom_call" | custom-call | flops 8589934592 | bytes 8388608 | tf_op jit(solution)/shard_map/attend/pallas_call | solution.py:268
  59.3 23.4 %all_to_all.15 = bf16[16,64,512]{2,1,0:T(8,128)(2,1)S(1)} all-to-all(bf16[16,64,512]{2,1,0:T(8,128)(2,1)S(1)} %bitcast.17), channel_id=1, replica_groups=mesh['ctx'=32,'uly'=16] {'uly'}, dimensions={0} | all-to-all | bytes 2097152 | tf_op jit(solution)/shard_map/all_to_all | solution.py:335
  82.7 1.1 %copy.24 = bf16[16,8,8,512]{3,2,0,1:T(8,128)(2,1)} copy(bf16[16,8,8,512]{3,2,1,0:T(8,128)(2,1)S(1)} %bitcast.22) | data formatting | bytes 2097152 | tf_op jit(solution)/shard_map/reshape | solution.py:336
  (19 shorter events, 0.1 us)
Async XLA Ops:
  0.0 1.0 %copy-start = (bf16[64,576]{1,0:T(8,128)(2,1)S(1)}, bf16[64,576]{1,0:T(8,128)(2,1)}, u32[]{:S(2)}) copy-start(bf16[64,576]{1,0:T(8,128)(2,1)} %latent_ref) | copy-start | bytes 221188
  0.3 0.8 copy-start.4
  1.1 8.8 %copy-start.3 = (bf16[64,12288]{1,0:T(8,128)(2,1)S(1)}, bf16[64,12288]{1,0:T(8,128)(2,1)}, u32[]{:S(2)}) copy-start(bf16[64,12288]{1,0:T(8,128)(2,1)} %param.9) | copy-start | bytes 4718596
  1.1 8.8 %copy-start.5 = (s32[128]{0:T(128)S(1)}, s32[128]{0:T(128)}, u32[]{:S(2)}) copy-start(s32[128]{0:T(128)} %param.13) | copy-start | bytes 1540
  2.2 22.9 %all-to-all-start.1 = ((bf16[16,288,128]{2,1,0:T(8,128)(2,1)}), bf16[16,288,128]{2,1,0:T(8,128)(2,1)}, u32[]{:S(2)}, u32[]{:S(2)}) async-start(bf16[16,288,128]{2,1,0:T(8,128)(2,1)} %spread.1), calls=%async_computation.1 | async-start | bytes 2359296 | tf_op jit(solution)/shard_map/all_to_all | solution.py:320
  25.1 24.5 %all-to-all-start = ((bf16[16,64,768]{2,1,0:T(8,128)(2,1)}), bf16[16,64,768]{2,1,0:T(8,128)(2,1)}, u32[]{:S(2)}, u32[]{:S(2)}) async-start(bf16[16,64,768]{2,1,0:T(8,128)(2,1)} %copy.20), calls=%async_computation | async-start | bytes 3145728 | tf_op jit(solution)/shard_map/all_to_all | solution.py:327
  30.6 19.1 %collective-permute-start = (bf16[16,288,128]{2,1,0:T(8,128)(2,1)}, bf16[16,288,128]{2,1,0:T(8,128)(2,1)S(1)}, u32[]{:S(2)}, u32[]{:S(2)}) collective-permute-start(bf16[16,288,128]{2,1,0:T(8,128)(2,1)} %all-to-all-done.1.packed_ref), channel_id=1, source_target_pairs={{16,32},{48,64},{80,96},{112,128},{144,160},{176,192},{208,224},{2... | collective-permute-start | bytes 3538952 | tf_op jit(solution)/shard_map/ppermute | solution.py:26
  33.2 16.5 %collective-permute-start.1 = (bf16[16,288,128]{2,1,0:T(8,128)(2,1)}, bf16[16,288,128]{2,1,0:T(8,128)(2,1)}, u32[]{:S(2)}, u32[]{:S(2)}) collective-permute-start(bf16[16,288,128]{2,1,0:T(8,128)(2,1)} %all-to-all-done.1.packed_ref), channel_id=1, source_target_pairs={{0,16},{32,48},{64,80},{96,112},{128,144},{160,176},{192,208},{224... | collective-permute-start | bytes 3538952 | tf_op jit(solution)/shard_map/ppermute | solution.py:26
  34.5 15.2 %copy-start.1 = (bf16[512,512]{1,0:T(8,128)(2,1)S(1)}, bf16[512,512]{1,0:T(8,128)(2,1)}, u32[]{:S(2)}) copy-start(bf16[512,512]{1,0:T(8,128)(2,1)} %key_up_hbm.1) | copy-start | bytes 1572868
  34.5 15.2 %copy-start.2 = (bf16[512,512]{1,0:T(8,128)(2,1)S(1)}, bf16[512,512]{1,0:T(8,128)(2,1)}, u32[]{:S(2)}) copy-start(bf16[512,512]{1,0:T(8,128)(2,1)} %value_up_hbm.1) | copy-start | bytes 1572868

commit v7 on v6

--- a/solution.py
+++ b/solution.py
@@ -175,12 +175,12 @@
 
     @pl.when(first_tile < tiles)
     def _():
-        for copy in lift_copies:
-            copy.start()
         for tile in range(tiles):
             needed = first_tile <= tile
             pl.when(needed & odd)(lambda tile=tile: prev_copy(near_hbm, tile).start())
             pl.when(needed & ~odd)(lambda tile=tile: prev_copy(far_hbm, tile).start())
+        for copy in lift_copies:
+            copy.start()
 
     code_copy.start()
     for tile in range(tiles):

time: 84 us -> 84.5 us (level)
  the two profiles are of different devices: /device:TPU:1 before, /device:TPU:96 now
where the time goes in v7:
time: 84.5 us; the launch traced here: 83.5 us
  blocking collectives  24.7 us (29%)
  starting transfers between devices  21.7 us (26%)
  Pallas kernels  15.2 us (18%)
  waiting for transfers between devices  12.4 us (15%)
  local copies, waits for them, and re-layouts  5.02 us (6%)
  other arithmetic  4.22 us (5%)
    all_to_all x1, blocking collectives, per_device(): result = lax.all_to_all(result, 'uly', split_axis=0, concat_axis=0)  24.7 us
    ppermute x2, starting transfers between devices, passed_along(): return lax.ppermute(block, axis, [(i, i + 1) for i in senders if i < last])  9.81 us
    pallas_call x1, Pallas kernels, attend(): pl.pallas_call(attend_kernel, in_specs=[pl.BlockSpec(memory_space=pltpu.S...  9.03 us
    all_to_all x1, starting transfers between devices, per_device(): lax.all_to_all(spread(latent, uly_count), 'uly', split_axis=0, concat_axi...  7.08 us
    all_to_all x1, waiting for transfers between devices, per_device(): lax.all_to_all(spread(latent, uly_count), 'uly', split_axis=0, concat_axi...  6.71 us
    all_to_all x1, waiting for transfers between devices, per_device(): local_query = lax.all_to_all(parts, 'uly', split_axis=0, concat_axis=0)  5.4 us
    pallas_call x1, Pallas kernels, lift(): pl.pallas_call(lift_kernel, grid=(steps,), in_specs=[packed_spec, tiled(2...  5.06 us
    all_to_all x1, starting transfers between devices, per_device(): local_query = lax.all_to_all(parts, 'uly', split_axis=0, concat_axis=0)  4.84 us
  transfers between devices with their start and end apart: 4, of which 3 were waited for; matrix products, arithmetic and copies ran while one was open for 9% of the time, Pallas kernels for 6%

profile of v7, /device:TPU:96, one launch (start us, length us, event | category | flops | bytes accessed | tf_op | source)
XLA Modules:
  0.0 83.5 jit_solution(13025580125021630853)
XLA Ops:
  0.0 0.2 conditional.2
  0.0 0.1 broadcast.325
  0.1 0.1 broadcast.327
  0.3 0.0 copy-start.4
  0.3 0.8 copy-done.4
  1.0 0.0 copy-done
  1.1 1.2 %spread.1 = bf16[16,288,128]{2,1,0:T(8,128)(2,1)} custom-call(bf16[64,576]{1,0:T(8,128)(2,1)S(1)} %copy-done), custom_call_target="tpu_custom_call" | custom-call | tf_op jit(solution)/shard_map/spread/pallas_call | solution.py:64
  2.2 7.1 %all-to-all-start.1 = ((bf16[16,288,128]{2,1,0:T(8,128)(2,1)}), bf16[16,288,128]{2,1,0:T(8,128)(2,1)}, u32[]{:S(2)}, u32[]{:S(2)}) async-start(bf16[16,288,128]{2,1,0:T(8,128)(2,1)} %spread.1), calls=%async_computation.1 | async-start | bytes 2359296 | tf_op jit(solution)/shard_map/all_to_all | solution.py:320
  9.3 5.6 %conditional.3 = (bf16[16,64,768]{2,0,1:T(8,128)(2,1)S(1)}, bf16[1024,128]{1,0:T(8,128)(2,1)S(1)}, s32[5]{0:T(128)S(1)}, bf16[1024,128]{1,0:T(8,128)(2,1)}, bf16[1024,128]{1,0:T(8,128)(2,1)}) conditional(s32[]{:T(128)} %convert_element_type.25, (bf16[64,12288]{1,0:T(8,128)(2,1)S(1)}, s32[128]{0:T(128)S(1)}, s32[]{:T(128)}, s32[]{:T(128)}) %tuple.42, ...), branch_computations={%region_5.9_spmd, %region_9.10_spmd} | conditional | flops 3997386 | bytes 5467588 | solution.py:321
  9.4 0.1 copy.19
  9.5 0.2 reduce-window.16
  9.6 0.1 reduce.1
  9.7 0.6 convert_reduce_fusion.1
  10.4 1.7 %select_convert_fusion.2 = bf16[2048,128]{1,0:T(8,128)(2,1)S(1)} fusion(pred[2048]{0:T(1024)(128)(4,1)S(1)} %broadcast_compare_fusion.1, pred[128]{0:T(512)(128)(4,1)S(1)} %and_or_fusion.1, s32[2048]{0:T(1024)S(1)} %get-tuple-element.100, s32[2048]{0:T(1024)S(1)} %get-tuple-element.99, s32[128]{0:T(128)S(1)} %and_select_fusion.3), kind=kLoop, calls=%fused_computation.24 | loop fusion | flops 2097152 | bytes 543360 | tf_op jit(solution)/shard_map/cond/branch_0_fun/convert_element_type | solution.py:39
  12.2 0.9 %fusion.7 = (bf16[1024,128]{1,0:T(8,128)(2,1)}, bf16[1024,128]{1,0:T(8,128)(2,1)}) fusion(bf16[2048,128]{1,0:T(8,128)(2,1)S(1)} %select_convert_fusion.2), kind=kLoop, calls=%fused_computation.49 | loop fusion | bytes 1048576 | tf_op jit(solution)/shard_map/slice | solution.py:329
  13.0 1.2 %compare_or_fusion.1 = pred[2048,128]{1,0:T(8,128)(4,1)S(1)} fusion(s32[128]{0:T(128)S(1)} %and_select_fusion.3, s32[2048]{0:T(1024)S(1)} %get-tuple-element.100, s32[2048]{0:T(1024)S(1)} %get-tuple-element.99), kind=kLoop, calls=%fused_computation.26 | loop fusion | flops 786432 | bytes 279040 | tf_op jit(solution)/shard_map/cond/branch_0_fun/or | solution.py:35
  14.2 0.1 select_convert_fusion.3
  14.3 0.2 select_reduce_fusion.1
  14.5 0.1 pad_add_fusion.1
  14.6 0.3 copy.23
  14.9 1.6 %copy.20 = bf16[16,64,768]{2,1,0:T(8,128)(2,1)} copy(bf16[16,64,768]{2,0,1:T(8,128)(2,1)S(1)} %get-tuple-element.88) | data formatting | bytes 3145728 | tf_op jit(solution)/shard_map/cond | solution.py:321
  16.6 6.7 %all-to-all-done.1.packed_ref = bf16[16,288,128]{2,1,0:T(8,128)(2,1)} async-done(((bf16[16,288,128]{2,1,0:T(8,128)(2,1)}), bf16[16,288,128]{2,1,0:T(8,128)(2,1)}, u32[]{:S(2)}, u32[]{:S(2)}) %all-to-all-start.1) | async-done | bytes 1179680 | tf_op jit(solution)/shard_map/all_to_all | solution.py:320
  23.3 4.8 %all-to-all-start = ((bf16[16,64,768]{2,1,0:T(8,128)(2,1)}), bf16[16,64,768]{2,1,0:T(8,128)(2,1)}, u32[]{:S(2)}, u32[]{:S(2)}) async-start(bf16[16,64,768]{2,1,0:T(8,128)(2,1)} %copy.20), calls=%async_computation | async-start | bytes 3145728 | tf_op jit(solution)/shard_map/all_to_all | solution.py:327
  28.1 1.3 %collective-permute-start = (bf16[16,288,128]{2,1,0:T(8,128)(2,1)}, bf16[16,288,128]{2,1,0:T(8,128)(2,1)S(1)}, u32[]{:S(2)}, u32[]{:S(2)}) collective-permute-start(bf16[16,288,128]{2,1,0:T(8,128)(2,1)} %all-to-all-done.1.packed_ref), channel_id=1, source_target_pairs={{16,32},{48,64},{80,96},{112,128},{144,160},{176,192},{208,224},{2... | collective-permute-start | bytes 3538952 | tf_op jit(solution)/shard_map/ppermute | solution.py:26
  29.4 8.5 %collective-permute-start.1 = (bf16[16,288,128]{2,1,0:T(8,128)(2,1)}, bf16[16,288,128]{2,1,0:T(8,128)(2,1)}, u32[]{:S(2)}, u32[]{:S(2)}) collective-permute-start(bf16[16,288,128]{2,1,0:T(8,128)(2,1)} %all-to-all-done.1.packed_ref), channel_id=1, source_target_pairs={{0,16},{32,48},{64,80},{96,112},{128,144},{160,176},{192,208},{224... | collective-permute-start | bytes 3538952 | tf_op jit(solution)/shard_map/ppermute | solution.py:26
  38.0 5.1 %lift.1.own_hbm = bf16[1024,1536]{1,0:T(8,128)(2,1)} custom-call(bf16[16,288,128]{2,1,0:T(8,128)(2,1)} %all-to-all-done.1.packed_ref, bf16[1024,128]{1,0:T(8,128)(2,1)} %get-tuple-element.92.code_ref, bf16[512,512]{1,0:T(8,128)(2,1)} %key_up_hbm.1, bf16[512,512]{1,0:T(8,128)(2,1)} %value_up_hbm.1), custom_call_target="tpu_custom_call" | custom-call | flops 1610612736 | bytes 4718592 | tf_op jit(solution)/shard_map/lift/pallas_call | solution.py:114
  43.0 5.4 %all-to-all-done = bf16[16,64,768]{2,1,0:T(8,128)(2,1)} async-done(((bf16[16,64,768]{2,1,0:T(8,128)(2,1)}), bf16[16,64,768]{2,1,0:T(8,128)(2,1)}, u32[]{:S(2)}, u32[]{:S(2)}) %all-to-all-start) | async-done | bytes 1572896 | tf_op jit(solution)/shard_map/all_to_all | solution.py:327
  48.4 0.3 collective-permute-done.far_hbm
  48.7 0.0 collective-permute-done.1.near_hbm
  48.7 9.0 %attend.1 = bf16[1024,512]{1,0:T(8,128)(2,1)S(1)} custom-call(s32[5]{0:T(128)S(1)} %get-tuple-element.87.first_ref, bf16[1024,768]{1,0:T(8,128)(2,1)} %bitcast.6.query_hbm, bf16[1024,128]{1,0:T(8,128)(2,1)S(1)} %get-tuple-element.89.code_hbm, bf16[16,288,128]{2,1,0:T(8,128)(2,1)S(1)} %collective-permute-done.far_hbm, ...), custom_call_target="tpu_custom_call" | custom-call | flops 8589934592 | bytes 8388608 | tf_op jit(solution)/shard_map/attend/pallas_call | solution.py:268
  57.8 24.7 %all_to_all.15 = bf16[16,64,512]{2,1,0:T(8,128)(2,1)S(1)} all-to-all(bf16[16,64,512]{2,1,0:T(8,128)(2,1)S(1)} %bitcast.17), channel_id=1, replica_groups=mesh['ctx'=32,'uly'=16] {'uly'}, dimensions={0} | all-to-all | bytes 2097152 | tf_op jit(solution)/shard_map/all_to_all | solution.py:335
  82.5 1.1 %copy.24 = bf16[16,8,8,512]{3,2,0,1:T(8,128)(2,1)} copy(bf16[16,8,8,512]{3,2,1,0:T(8,128)(2,1)S(1)} %bitcast.22) | data formatting | bytes 2097152 | tf_op jit(solution)/shard_map/reshape | solution.py:336
  (19 shorter events, 0.1 us)
Async XLA Ops:
  0.0 1.0 %copy-start = (bf16[64,576]{1,0:T(8,128)(2,1)S(1)}, bf16[64,576]{1,0:T(8,128)(2,1)}, u32[]{:S(2)}) copy-start(bf16[64,576]{1,0:T(8,128)(2,1)} %latent_ref) | copy-start | bytes 221188
  0.3 0.8 copy-start.4
  1.1 8.3 %copy-start.3 = (bf16[64,12288]{1,0:T(8,128)(2,1)S(1)}, bf16[64,12288]{1,0:T(8,128)(2,1)}, u32[]{:S(2)}) copy-start(bf16[64,12288]{1,0:T(8,128)(2,1)} %param.9) | copy-start | bytes 4718596
  1.1 8.3 %copy-start.5 = (s32[128]{0:T(128)S(1)}, s32[128]{0:T(128)}, u32[]{:S(2)}) copy-start(s32[128]{0:T(128)} %param.13) | copy-start | bytes 1540
  2.2 21.1 %all-to-all-start.1 = ((bf16[16,288,128]{2,1,0:T(8,128)(2,1)}), bf16[16,288,128]{2,1,0:T(8,128)(2,1)}, u32[]{:S(2)}, u32[]{:S(2)}) async-start(bf16[16,288,128]{2,1,0:T(8,128)(2,1)} %spread.1), calls=%async_computation.1 | async-start | bytes 2359296 | tf_op jit(solution)/shard_map/all_to_all | solution.py:320
  23.3 25.1 %all-to-all-start = ((bf16[16,64,768]{2,1,0:T(8,128)(2,1)}), bf16[16,64,768]{2,1,0:T(8,128)(2,1)}, u32[]{:S(2)}, u32[]{:S(2)}) async-start(bf16[16,64,768]{2,1,0:T(8,128)(2,1)} %copy.20), calls=%async_computation | async-start | bytes 3145728 | tf_op jit(solution)/shard_map/all_to_all | solution.py:327
  28.1 20.6 %collective-permute-start = (bf16[16,288,128]{2,1,0:T(8,128)(2,1)}, bf16[16,288,128]{2,1,0:T(8,128)(2,1)S(1)}, u32[]{:S(2)}, u32[]{:S(2)}) collective-permute-start(bf16[16,288,128]{2,1,0:T(8,128)(2,1)} %all-to-all-done.1.packed_ref), channel_id=1, source_target_pairs={{16,32},{48,64},{80,96},{112,128},{144,160},{176,192},{208,224},{2... | collective-permute-start | bytes 3538952 | tf_op jit(solution)/shard_map/ppermute | solution.py:26
  29.4 19.3 %collective-permute-start.1 = (bf16[16,288,128]{2,1,0:T(8,128)(2,1)}, bf16[16,288,128]{2,1,0:T(8,128)(2,1)}, u32[]{:S(2)}, u32[]{:S(2)}) collective-permute-start(bf16[16,288,128]{2,1,0:T(8,128)(2,1)} %all-to-all-done.1.packed_ref), channel_id=1, source_target_pairs={{0,16},{32,48},{64,80},{96,112},{128,144},{160,176},{192,208},{224... | collective-permute-start | bytes 3538952 | tf_op jit(solution)/shard_map/ppermute | solution.py:26
  38.0 10.7 %copy-start.1 = (bf16[512,512]{1,0:T(8,128)(2,1)S(1)}, bf16[512,512]{1,0:T(8,128)(2,1)}, u32[]{:S(2)}) copy-start(bf16[512,512]{1,0:T(8,128)(2,1)} %key_up_hbm.1) | copy-start | bytes 1572868
  38.0 10.8 %copy-start.2 = (bf16[512,512]{1,0:T(8,128)(2,1)S(1)}, bf16[512,512]{1,0:T(8,128)(2,1)}, u32[]{:S(2)}) copy-start(bf16[512,512]{1,0:T(8,128)(2,1)} %value_up_hbm.1) | copy-start | bytes 1572868
